TPU v7x, 32 devices: a whole 2x2x4 slice. The times are simulated.
32 devices in a mesh: grp: 4 (over y, core), dev: 8 (over z, x).
Axes of the slice: x: 2, y: 2, z: 4, core: 2. Of those that a mesh axis runs over, the one named last changes fastest.
Arguments:
- residual_edges: float32 [16, 172032], P(None, ('grp', 'dev')), may hold values from -6 to 6
- pi_block: float32 [144, 192], replicated, may hold values from -0.4375 to 0.4375
- stiff_block: float32 [64, 64], replicated, may hold values from -0.05 to 5.15, as said below
- mass_block: float32 [64, 64], replicated, may hold values from -0.03 to 3.89, as said below
- permittivity: float32 [6, 2048], P(None, ('grp', 'dev')), may hold values from -1.6 to 4, as said below
- curl_coef: float32 [2048], P(('grp', 'dev')), may hold values from 0.02 to 2
- edge_map: int32 [144, 2048], P(None, ('grp', 'dev')), may hold values from 0 to 6719, as said below
- local_map: int32 [64, 2048], P(None, ('grp', 'dev')), may hold values from 0 to 2047
- node_owner: int32 [65536], P(('grp', 'dev')), may hold values from 0 to 7, as said below
- node_slot: int32 [65536], P(('grp', 'dev')), may hold values from 0 to 1727
Outputs:
- correction: float32 [16, 172032], P(None, ('grp', 'dev'))
Inputs may be any that keep to these rules, and one draw needn't show every extreme that they name: `edge_map`: entries of one device's elements (aligned blocks of 64 columns) below 672 or at 6048 or above occur only where the neighbouring block along grp+dev order exists; both ends of the range are reached wherever that neighbour exists. `node_owner`: among the 2048 touched nodes of one device at most 512 have the same owner; in every group one owner has exactly 512 from every device of that group. `stiff_block`: Symmetric; diagonal entries between 4.15 and 5.15, the others within 0.05 of zero. `mass_block`: Symmetric; diagonal entries between 2.89 and 3.89, the others within 0.03 of zero. `permittivity`: rows 0 to 2 lie between 0.05 and 4; rows 3 to 5 within 1.6 of zero.
All inputs are finite; a program needn't handle non-finite values.
Results may differ from a plain program's by a relative error of at most 0.0003.
Values sent between devices are 32-bit elements; how exact they have to be, the bound alone decides.
A program may use at most 128 MiB of HBM per device.

v0:
```python
import functools
import jax
import jax.numpy as jnp
from jax import lax
from jax.experimental import pallas as pl
from jax.experimental.pallas import tpu as pltpu
from jax.sharding import PartitionSpec as P

N_LOC = 1728
CHUNK = 256
WIDE = 512
F32 = jnp.float32
BF16 = jnp.bfloat16
AUX = 8
CHEB_LOW = 0.3
CHEB_HIGH = 2.0
VMEM_BYTES = 50 * 1024 * 1024


def cheb_factors():
    center = 0.5 * (CHEB_HIGH + CHEB_LOW)
    half_width = 0.5 * (CHEB_HIGH - CHEB_LOW)
    sigma_ratio = center / half_width
    rho_first = 1.0 / sigma_ratio
    rho_second = 1.0 / (2.0 * sigma_ratio - rho_first)
    return (1.0 / center, 1.0 + rho_second * rho_first, 2.0 * rho_second / half_width)


def iota(shape, dim):
    return lax.broadcasted_iota(jnp.int32, shape, dim)


def dot(a, b):
    return lax.dot_general(a, b, (((1,), (0,)), ((), ())), preferred_element_type=F32)


def dot_nt(a, b):
    return lax.dot_general(a, b, (((1,), (1,)), ((), ())), preferred_element_type=F32)


def split(x):
    high = x.astype(BF16)
    low = (x - high.astype(F32)).astype(BF16)
    return high, low


def split_wide(x):
    high, low = split(x)
    return jnp.concatenate([high, low], axis=1)


def ones_where(mask):
    return jnp.where(mask, 1.0, 0.0).astype(BF16)


def onehot(low_index):
    return ones_where(iota((CHUNK, low_index.shape[1]), 0) == low_index)


def gather_cols(table2, high_index, hot, groups, rows):
    found = dot(table2, jnp.concatenate([hot, hot], axis=0))
    picked = jnp.zeros((rows, hot.shape[1]), F32)
    for h in range(groups):
        picked = jnp.where(high_index == h, found[h * rows : (h + 1) * rows], picked)
    return picked


def scatter_cols(values, high_index, hot, groups):
    high, low = split(values)
    high, low = high.astype(F32), low.astype(F32)
    masks = [high_index == h for h in range(groups)]
    high_rows = jnp.concatenate([jnp.where(m, high, 0.0) for m in masks], axis=0)
    low_rows = jnp.concatenate([jnp.where(m, low, 0.0) for m in masks], axis=0)
    both = jnp.concatenate([high_rows.astype(BF16), low_rows.astype(BF16)], axis=1)
    return dot_nt(both, jnp.concatenate([hot, hot], axis=1))


def dot3(x, w_high, w_low):
    high, low = split(x)
    return dot(high, w_high) + dot(low, w_high) + dot(high, w_low)


def dot3_nt(x, w_high, w_low):
    high, low = split(x)
    return dot_nt(high, w_high) + dot_nt(low, w_high) + dot_nt(high, w_low)


def block_weights(block, copies):
    size = block.shape[0]
    total = size * copies
    spread = ones_where(iota((size, total), 1) % size == iota((size, total), 0))
    keep = iota((total, total), 0) // size == iota((total, total), 1) // size
    out = []
    for part in split(block):
        row = dot(part, spread)
        full = jnp.concatenate([row] * copies, axis=0)
        out.append(jnp.where(keep, full, 0.0).astype(BF16))
    return out


def pi_weights(pi_rows, copies, nodes):
    count, total = pi_rows.shape
    comps = total // nodes
    width = comps * copies * nodes
    col, row = iota((total, width), 1), iota((total, width), 0)
    per = copies * nodes
    spread = ones_where((col // per == row // nodes) & (col % nodes == row % nodes))
    shape = (copies * count, width)
    keep = iota(shape, 0) // count == (iota(shape, 1) % per) // nodes
    out = []
    for part in split(pi_rows):
        one = dot(part, spread)
        full = jnp.concatenate([one] * copies, axis=0)
        out.append(jnp.where(keep, full, 0.0).astype(BF16))
    return out


def prepare_weights(pi_ref, stiff_ref, mass_ref, wa, wb, ws, wm):
    nodes = stiff_ref.shape[0]
    for ref, parts in (
        (wa, pi_weights(pi_ref[:128], 2, nodes)),
        (wb, pi_weights(pi_ref[128:], 8, nodes)),
        (ws, block_weights(stiff_ref[...], 4)),
        (wm, block_weights(mass_ref[...], 4)),
    ):
        ref[0] = parts[0]
        ref[1] = parts[1]


def prepare_coefs(coef_ref, stiff_ref, mass_ref, coef_q, diag_q):
    nodes = stiff_ref.shape[0]
    eye = iota((nodes, nodes), 0) == iota((nodes, nodes), 1)
    sd = jnp.sum(jnp.where(eye, stiff_ref[...], 0.0), axis=0, keepdims=True)
    md = jnp.sum(jnp.where(eye, mass_ref[...], 0.0), axis=0, keepdims=True)
    diags = jnp.concatenate([sd, md, jnp.zeros((6, nodes), F32)], axis=0)
    d_parts = split(diags)
    c_parts = split(coef_ref[...])
    elems = coef_ref.shape[1]

    def body(i, _):
        lane = iota((elems, WIDE), 1) + i * WIDE
        by_elem = ones_where(lane // nodes == iota((elems, WIDE), 0))
        lane_n = iota((nodes, WIDE), 1)
        by_node = ones_where(lane_n % nodes == iota((nodes, WIDE), 0))
        coef = dot(c_parts[0], by_elem) + dot(c_parts[1], by_elem)
        diag = dot(d_parts[0], by_node) + dot(d_parts[1], by_node)
        at = pl.ds(pl.multiple_of(i * WIDE, WIDE), WIDE)
        coef_q[:, at] = coef
        base = coef[0:1] * diag[0:1]
        rows = iota((AUX, WIDE), 0)
        terms = jnp.zeros((AUX, WIDE), F32)
        for c in range(3):
            terms = jnp.where(rows == c, base + diag[1:2] * coef[1 + c : 2 + c], terms)
        diag_q[:, at] = terms
        return 0

    lax.fori_loop(0, coef_q.shape[1] // WIDE, body, 0)


def prepare_places(peers, owner_ref, slot_ref, local_ref, pos_hi, pos_lo, slot_buf):
    touched = owner_ref.shape[1]
    capacity = 2 * touched // peers
    groups = 2 * touched // CHUNK
    tri = ones_where(iota((CHUNK, CHUNK), 0) < iota((CHUNK, CHUNK), 1))
    carry = jnp.zeros((peers, 1), F32)
    place = []
    for i in range(touched // CHUNK):
        own = owner_ref[:, i * CHUNK : (i + 1) * CHUNK]
        hot = jnp.where(iota((peers, CHUNK), 0) == own, 1.0, 0.0)
        before = dot(hot.astype(BF16), tri) + carry
        rank = jnp.sum(hot * before, axis=0, keepdims=True)
        carry = carry + jnp.sum(hot, axis=1, keepdims=True)
        place.append(own * capacity + rank.astype(jnp.int32))
    rows8 = iota((AUX, CHUNK), 0)
    table_hi = jnp.zeros((AUX, CHUNK), F32)
    table_lo = jnp.zeros((AUX, CHUNK), F32)
    slots = jnp.zeros((2 * groups, CHUNK), F32)
    for i, pos in enumerate(place):
        high, low = pos // CHUNK, pos % CHUNK
        table_hi = jnp.where(rows8 == i, high.astype(F32), table_hi)
        table_lo = jnp.where(rows8 == i, low.astype(F32), table_lo)
        slot = slot_ref[:, i * CHUNK : (i + 1) * CHUNK] + 1
        here = iota((groups, CHUNK), 0) == high
        s_hi = jnp.where(here, (slot // CHUNK).astype(F32), 0.0)
        s_lo = jnp.where(here, (slot % CHUNK).astype(F32), 0.0)
        both = jnp.concatenate([s_hi, s_lo], axis=0).astype(BF16)
        slots = slots + dot_nt(both, onehot(low))
    slot_buf[...] = slots[:groups] * float(CHUNK) + slots[groups:]
    table = jnp.concatenate([table_hi, table_lo], axis=0).astype(BF16)

    def body(i, _):
        at = pl.ds(pl.multiple_of(i * WIDE, WIDE), WIDE)
        local = local_ref[:, at]
        found = dot(table, onehot(local % CHUNK))
        here = iota((AUX, WIDE), 0) == local // CHUNK
        high = jnp.sum(jnp.where(here, found[:AUX], 0.0), axis=0, keepdims=True)
        low = jnp.sum(jnp.where(here, found[AUX:], 0.0), axis=0, keepdims=True)
        pos_hi[:, at] = high.astype(jnp.int32)
        pos_lo[:, at] = low.astype(jnp.int32)
        return 0

    lax.fori_loop(0, local_ref.shape[1] // WIDE, body, 0)


def edge_gather(table2, emap_ref, rhs, xa, xb):
    groups = table2.shape[0] // rhs
    a_chunks = xa.shape[0] // rhs * CHUNK // WIDE

    def take(i):
        at = pl.ds(pl.multiple_of(i * WIDE, WIDE), WIDE)
        index = emap_ref[:, at]
        return gather_cols(table2[...], index // CHUNK, onehot(index % CHUNK), groups, rhs)

    def body(i, _):
        got = take(i)
        for s in range(2):
            at = pl.multiple_of((2 * i + s) * rhs, rhs)
            xa[pl.ds(at, rhs), :] = got[:, s * CHUNK : (s + 1) * CHUNK]
        return 0

    lax.fori_loop(0, a_chunks, body, 0)
    for i in range(2):
        got = take(a_chunks + i)
        for s in range(4):
            xb[(4 * i + s) * rhs : (4 * i + s + 1) * rhs, :] = got[:, s * 128 : (s + 1) * 128]


def restrict(xa, xb, wa, wb, rhs, terms):
    ya = dot3(xa[...], wa[0], wa[1])
    yb = dot3(xb[...], wb[0], wb[1])
    for p in range(xa.shape[0] // rhs):
        for c in range(3):
            first = ya[p * rhs : (p + 1) * rhs, c * 128 : (c + 1) * 128]
            lane = c * 512 + (p % 4) * 128
            second = yb[(p // 4) * rhs : (p // 4 + 1) * rhs, lane : lane + 128]
            terms[c * rhs : (c + 1) * rhs, p * 128 : (p + 1) * 128] = first + second


def scatter_elems(terms, pos_hi, pos_lo, acc):
    rows, total = terms.shape
    groups = acc.shape[0] // rows
    acc[...] = jnp.zeros_like(acc)

    def body(i, _):
        at = pl.ds(pl.multiple_of(i * WIDE, WIDE), WIDE)
        acc[...] += scatter_cols(terms[:, at], pos_hi[:, at], onehot(pos_lo[:, at]), groups)
        return 0

    lax.fori_loop(0, total // WIDE, body, 0)


def lay_out(send, acc, rows, first_row):
    capacity = send.shape[2]
    for h in range(acc.shape[0] // rows):
        step = min(capacity, CHUNK)
        for s in range(CHUNK // step):
            lane = h * CHUNK + s * step
            peer, off = lane // capacity, lane % capacity
            send[peer, first_row : first_row + rows, off : off + step] = acc[
                h * rows : (h + 1) * rows, s * step : (s + 1) * step
            ]


def table_from(got, rows, table2):
    peers, _, capacity = got.shape
    for h in range(peers * capacity // CHUNK):
        step = min(capacity, CHUNK)
        parts = []
        for s in range(CHUNK // step):
            lane = h * CHUNK + s * step
            peer, off = lane // capacity, lane % capacity
            parts.append(got[peer, :rows, off : off + step])
        value = parts[0] if len(parts) == 1 else jnp.concatenate(parts, axis=1)
        table2[h * rows : (h + 1) * rows, :] = split_wide(value)


def gather_elems(table2, pos_hi, pos_lo, rows, visit):
    groups = table2.shape[0] // rows

    def body(i, _):
        at = pl.ds(pl.multiple_of(i * WIDE, WIDE), WIDE)
        visit(i, gather_cols(table2[...], pos_hi[:, at], onehot(pos_lo[:, at]), groups, rows))
        return 0

    lax.fori_loop(0, pos_hi.shape[1] // WIDE, body, 0)


def home_index(slot_row):
    slot = slot_row.astype(jnp.int32) - 1
    return jnp.where(slot < 0, -1, slot // CHUNK), jnp.maximum(slot, 0) % CHUNK


def sum_home(got, slots, first_row, rows, acc):
    groups = acc.shape[0] // rows
    acc[...] = jnp.zeros_like(acc)

    def body(p, _):
        high, low = home_index(slots[p])
        values = got[p, first_row : first_row + rows, :]
        acc[...] += scatter_cols(values, high, onehot(low), groups)
        return 0

    lax.fori_loop(0, got.shape[0], body, 0)


def fetch_home(table2, slots, rows, send):
    groups = table2.shape[0] // rows

    def body(p, _):
        high, low = home_index(slots[p])
        send[p] = gather_cols(table2[...], high, onehot(low), groups, rows)
        return 0

    lax.fori_loop(0, send.shape[0], body, 0)


def apply_operator(x_all, ws, wm, coef_q, rhs, terms):
    rows = 3 * rhs
    stiff = dot3(x_all[...], ws[0], ws[1])
    mass = dot3(x_all[...], wm[0], wm[1])
    tensor = ((1, 4, 5), (4, 2, 6), (5, 6, 3))
    for i in range(x_all.shape[0] // rows):
        lanes = slice(i * CHUNK, (i + 1) * CHUNK)
        coef = coef_q[:, lanes]
        for c in range(3):
            at = i * rows + c * rhs
            total = coef[0:1] * stiff[at : at + rhs]
            for c2 in range(3):
                t = tensor[c][c2]
                at2 = i * rows + c2 * rhs
                total = total + coef[t : t + 1] * mass[at2 : at2 + rhs]
            terms[c * rhs : (c + 1) * rhs, lanes] = total


def edge_scatter(ea, eb, emap_ref, rhs, acc):
    groups = acc.shape[0] // rhs
    a_chunks = ea.shape[0] // rhs * CHUNK // WIDE
    acc[...] = jnp.zeros_like(acc)

    def put(i, values):
        at = pl.ds(pl.multiple_of(i * WIDE, WIDE), WIDE)
        index = emap_ref[:, at]
        acc[...] += scatter_cols(values, index // CHUNK, onehot(index % CHUNK), groups)

    def body(i, _):
        parts = [ea[pl.ds(pl.multiple_of((2 * i + s) * rhs, rhs), rhs), :] for s in range(2)]
        put(i, jnp.concatenate(parts, axis=1))
        return 0

    lax.fori_loop(0, a_chunks, body, 0)
    for i in range(2):
        parts = [eb[(4 * i + s) * rhs : (4 * i + s + 1) * rhs, :] for s in range(4)]
        put(a_chunks + i, jnp.concatenate(parts, axis=1))


def restrict_kernel(
    peers, res, before, after, emap, local, owner, slot, coef, pi, stiff, mass,
    send, pos_hi, pos_lo, coef_q, wa, wb, ws, wm,
    table2, xa, xb, terms, diag_q, acc, acc_d, slot_buf,
):
    rhs = res.shape[0]
    prepare_weights(pi, stiff, mass, wa, wb, ws, wm)
    prepare_coefs(coef, stiff, mass, coef_q, diag_q)
    prepare_places(peers, owner, slot, local, pos_hi, pos_lo, slot_buf)
    h = 0
    for ref in (res, before, after):
        for i in range(ref.shape[1] // CHUNK):
            table2[h * rhs : (h + 1) * rhs, :] = split_wide(ref[:, i * CHUNK : (i + 1) * CHUNK])
            h += 1
    edge_gather(table2, emap, rhs, xa, xb)
    restrict(xa, xb, wa, wb, rhs, terms)
    scatter_elems(terms, pos_hi, pos_lo, acc)
    scatter_elems(diag_q, pos_hi, pos_lo, acc_d)
    for g in range(slot_buf.shape[0]):
        acc_d[g * AUX + 3 : g * AUX + 4, :] = slot_buf[g : g + 1, :]
    lay_out(send, acc, 3 * rhs, 0)
    lay_out(send, acc_d, AUX, 3 * rhs)


def first_home(got, send, slots, rhs_nodes, floored, acc_d, table2):
    rows = send.shape[1]
    rhs = rows // 3
    first = cheb_factors()[0]
    slots[...] = got[:, rows + 3 : rows + 4, :]
    sum_home(got, slots, 0, rows, rhs_nodes)
    sum_home(got, slots, rows, AUX, acc_d)
    floored[...] = jnp.maximum(acc_d[...], 1.0)
    for h in range(rhs_nodes.shape[0] // rows):
        for c in range(3):
            at = slice(h * rows + c * rhs, h * rows + (c + 1) * rhs)
            weight = floored[h * AUX + c : h * AUX + c + 1, :]
            table2[at, :] = split_wide(first * rhs_nodes[at, :] / weight)
    fetch_home(table2, slots, rows, send)


def second_home(got, slots, rhs_nodes, floored, send, acc, table2):
    rows = send.shape[1]
    rhs = rows // 3
    first, keep, step = cheb_factors()
    sum_home(got, slots, 0, rows, acc)
    for h in range(rhs_nodes.shape[0] // rows):
        for c in range(3):
            at = slice(h * rows + c * rhs, h * rows + (c + 1) * rhs)
            weight = floored[h * AUX + c : h * AUX + c + 1, :]
            nodes = rhs_nodes[at, :]
            value = keep * (first * nodes / weight) + step * (nodes - acc[at, :]) / weight
            table2[at, :] = split_wide(value)
    fetch_home(table2, slots, rows, send)


def operate_kernel(got, pos_hi, pos_lo, coef_q, ws, wm, send, table2, x_all, terms, acc):
    rows = send.shape[1]
    table_from(got, rows, table2)

    def visit(i, value):
        for s in range(2):
            at = pl.multiple_of((2 * i + s) * rows, rows)
            x_all[pl.ds(at, rows), :] = value[:, s * CHUNK : (s + 1) * CHUNK]

    gather_elems(table2, pos_hi, pos_lo, rows, visit)
    apply_operator(x_all, ws, wm, coef_q, rows // 3, terms)
    scatter_elems(terms, pos_hi, pos_lo, acc)
    lay_out(send, acc, rows, 0)


def prolong_kernel(
    got, pos_hi, pos_lo, emap, wa, wb, own, before, after, table2, xa, xb, ea, eb, acc
):
    rows = got.shape[1]
    rhs = rows // 3
    table_from(got, rows, table2)

    def visit(i, value):
        for c in range(3):
            part = value[c * rhs : (c + 1) * rhs]
            xb[pl.ds(pl.multiple_of(i * rhs, rhs), rhs), c * WIDE : (c + 1) * WIDE] = part
            for s in range(4):
                at = pl.multiple_of((4 * i + s) * rhs, rhs)
                xa[pl.ds(at, rhs), c * 128 : (c + 1) * 128] = part[:, s * 128 : (s + 1) * 128]

    gather_elems(table2, pos_hi, pos_lo, rows, visit)
    ea[...] = dot3_nt(xa[...], wa[0], wa[1])
    eb[...] = dot3_nt(xb[...], wb[0], wb[1])
    edge_scatter(ea, eb, emap, rhs, acc)
    h = 0
    for ref in (own, before, after):
        for i in range(ref.shape[1] // CHUNK):
            ref[:, i * CHUNK : (i + 1) * CHUNK] = acc[h * rhs : (h + 1) * rhs, :]
            h += 1


def call(body, outs, scratch, *args):
    vmem = pl.BlockSpec(memory_space=pltpu.VMEM)
    return pl.pallas_call(
        body,
        out_shape=[jax.ShapeDtypeStruct(*o) for o in outs],
        in_specs=[vmem] * len(args),
        out_specs=[vmem] * len(outs),
        scratch_shapes=[pltpu.VMEM(*s) for s in scratch],
        compiler_params=pltpu.CompilerParams(vmem_limit_bytes=VMEM_BYTES),
    )(*args)


def shifted(array, width_axes, up):
    size = lax.axis_size(width_axes)
    pairs = [(i, i + 1) for i in range(size - 1)]
    return lax.ppermute(array, width_axes, pairs if up else [(j, i) for i, j in pairs])


def per_device(
    residual, pi, stiff, mass, permittivity, curl, edge_map, local_map, node_owner, node_slot
):
    rhs, edges = residual.shape
    ed, elems = edge_map.shape
    nodes = local_map.shape[0]
    touched = node_owner.shape[0]
    peers = lax.axis_size("dev")
    capacity = 2 * touched // peers
    rim = edges // 8
    rim_pad = -(-rim // CHUNK) * CHUNK
    rows = 3 * rhs
    entries = nodes * elems
    e_entries = ed * elems
    axes = ("grp", "dev")
    pad = ((0, 0), (0, rim_pad - rim))
    before = jnp.pad(shifted(residual[:, edges - rim :], axes, True), pad)
    after = jnp.pad(shifted(residual[:, :rim], axes, False), pad)
    place = edge_map.T - rim
    place = jnp.where(
        place < 0,
        place + rim + edges,
        jnp.where(place >= edges, place + rim_pad, place),
    )
    emap = jnp.concatenate([place[:, :128].reshape(1, -1), place[:, 128:].reshape(1, -1)], axis=1)
    local = local_map.T.reshape(1, -1)
    coef = jnp.concatenate([curl[None], permittivity, jnp.zeros((1, elems), F32)], axis=0)
    groups = 2 * touched // CHUNK
    home = -(-N_LOC // CHUNK)
    e_groups = (edges + 2 * rim_pad) // CHUNK
    pairs = elems // 2
    buffer = ((peers, rows, capacity), F32)
    wa_shape, wb_shape = ((2, 256, 384), BF16), ((2, 128, 1536), BF16)
    ws_shape = ((2, CHUNK, CHUNK), BF16)
    send, pos_hi, pos_lo, coef_q, wa, wb, ws, wm = call(
        functools.partial(restrict_kernel, peers),
        [
            ((peers, rows + AUX, capacity), F32),
            ((1, entries), jnp.int32),
            ((1, entries), jnp.int32),
            ((AUX, entries), F32),
            wa_shape, wb_shape, ws_shape, ws_shape,
        ],
        [
            ((e_groups * rhs, 2 * CHUNK), BF16),
            ((pairs * rhs, 256), F32),
            ((elems // 8 * rhs, 128), F32),
            ((rows, entries), F32),
            ((AUX, entries), F32),
            ((groups * rows, CHUNK), F32),
            ((groups * AUX, CHUNK), F32),
            ((groups, CHUNK), F32),
        ],
        residual, before, after, emap, local, node_owner[None], node_slot[None], coef, pi, stiff,
        mass,
    )

    def exchange(array):
        return lax.all_to_all(array, "dev", split_axis=0, concat_axis=0, tiled=True)

    send, slots, rhs_nodes, floored = call(
        first_home,
        [
            buffer,
            ((peers, 1, capacity), F32),
            ((home * rows, CHUNK), F32),
            ((home * AUX, CHUNK), F32),
        ],
        [((home * AUX, CHUNK), F32), ((home * rows, 2 * CHUNK), BF16)],
        exchange(send),
    )
    (send,) = call(
        operate_kernel,
        [buffer],
        [
            ((groups * rows, 2 * CHUNK), BF16),
            ((entries // CHUNK * rows, CHUNK), F32),
            ((rows, entries), F32),
            ((groups * rows, CHUNK), F32),
        ],
        exchange(send), pos_hi, pos_lo, coef_q, ws, wm,
    )
    (send,) = call(
        second_home,
        [buffer],
        [((home * rows, CHUNK), F32), ((home * rows, 2 * CHUNK), BF16)],
        exchange(send), slots, rhs_nodes, floored,
    )
    own, to_before, to_after = call(
        prolong_kernel,
        [((rhs, edges), F32), ((rhs, rim_pad), F32), ((rhs, rim_pad), F32)],
        [
            ((groups * rows, 2 * CHUNK), BF16),
            ((pairs * rhs, 384), F32),
            ((elems // 8 * rhs, 1536), F32),
            ((pairs * rhs, 256), F32),
            ((elems // 8 * rhs, 128), F32),
            ((e_groups * rhs, CHUNK), F32),
        ],
        exchange(send), pos_hi, pos_lo, emap, wa, wb,
    )
    from_after = shifted(to_before[:, :rim], axes, False)
    from_before = shifted(to_after[:, :rim], axes, True)
    own = own.at[:, :rim].add(from_before)
    return own.at[:, edges - rim :].add(from_after)


def solution(mesh):
    both = ("grp", "dev")
    in_specs = (
        P(None, both), P(), P(), P(), P(None, both), P(both), P(None, both), P(None, both),
        P(both), P(both),
    )
    return jax.shard_map(
        per_device, mesh=mesh, in_specs=in_specs, out_specs=P(None, both), check_vma=False
    )
```

profile of v0, /device:TPU:0, one launch (start us, length us, event | category | flops | bytes accessed | tf_op | source)
XLA Modules:
  0.0 185.3 jit_solution(3571759399703514673)
XLA Ops:
  0.0 0.9 fusion.1
  0.9 4.8 %collective-permute-start = (f32[16,672]{1,0:T(8,128)S(1)}, f32[16,672]{1,0:T(8,128)S(1)}, u32[]{:S(2)}, u32[]{:S(2)}) collective-permute-start(f32[16,672]{1,0:T(8,128)S(1)} %get-tuple-element.60), channel_id=1, source_target_pairs={{0,1},{1,2},{2,3},{3,4},{4,5},{5,6},{6,7},{7,8},{8,9},{9,10},{10,1... | collective-permute-start | bytes 129032 | tf_op jit(solution)/shard_map/ppermute | solution.py:467
  5.8 1.4 collective-permute-start.1
  7.5 0.5 copy-done.9
  7.9 0.1 copy-done.8
  8.4 3.7 %collective-permute-done.1 = f32[16,672]{1,0:T(8,128)S(1)} collective-permute-done((f32[16,672]{1,0:T(8,128)S(1)}, f32[16,672]{1,0:T(8,128)S(1)}, u32[]{:S(2)}, u32[]{:S(2)}) %collective-permute-start.1) | collective-permute-done | bytes 43040 | tf_op jit(solution)/shard_map/ppermute | solution.py:467
  12.1 0.6 copy-done.4
  12.8 19.7 %shard_map.100 = (f32[8,56,512]{2,1,0:T(8,128)S(1)}, s32[1,4096]{1,0:T(1,128)S(1)}, s32[1,4096]{1,0:T(1,128)S(1)}, f32[8,4096]{1,0:T(8,128)S(1)}, bf16[2,256,384...) custom-call(f32[16,5376]{1,0:T(8,128)S(1)} %copy-done, ...), custom_call_target="tpu_custom_call" | custom-call | tf_op jit(solution)/shard_map/pallas_call | solution.py:454
  32.5 29.5 %all_to_all.20.got = f32[8,56,512]{2,1,0:T(8,128)S(1)} all-to-all(f32[8,56,512]{2,1,0:T(8,128)S(1)} %get-tuple-element.44), channel_id=1, replica_groups=mesh['grp'=4,'dev'=8] {'dev'}, dimensions={0} | all-to-all | bytes 1835008 | tf_op jit(solution)/shard_map/all_to_all | solution.py:528
  62.0 8.7 %shard_map.101 = (f32[8,48,512]{2,1,0:T(8,128)S(1)}, f32[8,1,512]{2,1,0:T(1,128)S(1)}, f32[336,256]{1,0:T(8,128)S(1)}, f32[56,256]{1,0:T(8,128)S(1)}) custom-call(f32[8,56,512]{2,1,0:T(8,128)S(1)} %all_to_all.20.got), custom_call_target="tpu_custom_call" | custom-call | tf_op jit(solution)/shard_map/pallas_call | solution.py:454
  70.7 24.5 %all_to_all.21.got = f32[8,48,512]{2,1,0:T(8,128)S(1)} all-to-all(f32[8,48,512]{2,1,0:T(8,128)S(1)} %get-tuple-element.45), channel_id=1, replica_groups=mesh['grp'=4,'dev'=8] {'dev'}, dimensions={0} | all-to-all | bytes 1572864 | tf_op jit(solution)/shard_map/all_to_all | solution.py:528
  95.2 10.7 %shard_map.102 = f32[8,48,512]{2,1,0:T(8,128)S(1)} custom-call(f32[8,48,512]{2,1,0:T(8,128)S(1)} %all_to_all.21.got, s32[1,4096]{1,0:T(1,128)S(1)} %get-tuple-element.46.pos_hi, s32[1,4096]{1,0:T(1,128)S(1)} %get-tuple-element.47.pos_lo, f32[8,4096]{1,0:T(8,128)S(1)} %get-tuple-element.48.coef_q, bf16[2,256,256]{2,1,0:T(8,128)(2,1)S(1)} %get-tuple-element.49.ws, ...), custom_call_target="tpu_custom_call" | custom-call | tf_op jit(solution)/shard_map/pallas_call | solution.py:454
  105.9 23.2 %all_to_all.22.got = f32[8,48,512]{2,1,0:T(8,128)S(1)} all-to-all(f32[8,48,512]{2,1,0:T(8,128)S(1)} %shard_map.102), channel_id=1, replica_groups=mesh['grp'=4,'dev'=8] {'dev'}, dimensions={0} | all-to-all | bytes 1572864 | tf_op jit(solution)/shard_map/all_to_all | solution.py:528
  129.1 6.4 %shard_map.103 = f32[8,48,512]{2,1,0:T(8,128)S(1)} custom-call(f32[8,48,512]{2,1,0:T(8,128)S(1)} %all_to_all.22.got, f32[8,1,512]{2,1,0:T(1,128)S(1)} %get-tuple-element.51.slots, f32[336,256]{1,0:T(8,128)S(1)} %get-tuple-element.52.rhs_nodes, f32[56,256]{1,0:T(8,128)S(1)} %get-tuple-element.53.floored), custom_call_target="tpu_custom_call" | custom-call | tf_op jit(solution)/shard_map/pallas_call | solution.py:454
  135.6 23.0 %all_to_all.23.got = f32[8,48,512]{2,1,0:T(8,128)S(1)} all-to-all(f32[8,48,512]{2,1,0:T(8,128)S(1)} %shard_map.103), channel_id=1, replica_groups=mesh['grp'=4,'dev'=8] {'dev'}, dimensions={0} | all-to-all | bytes 1572864 | tf_op jit(solution)/shard_map/all_to_all | solution.py:528
  158.6 14.4 %shard_map.104 = (f32[16,5376]{1,0:T(8,128)}, f32[16,768]{1,0:T(8,128)S(1)}, f32[16,768]{1,0:T(8,128)S(1)}) custom-call(f32[8,48,512]{2,1,0:T(8,128)S(1)} %all_to_all.23.got, s32[1,4096]{1,0:T(1,128)S(1)} %get-tuple-element.46.pos_hi, s32[1,4096]{1,0:T(1,128)S(1)} %get-tuple-element.47.pos_lo, s32[1,9216]{1,0:T(1,128)S(1)} %pad_add_fusion.emap, ...), custom_call_target="tpu_custom_call" | custom-call | tf_op jit(solution)/shard_map/pallas_call | solution.py:454
  172.9 3.3 %collective-permute-start.2 = (f32[16,672]{1,0:T(8,128)S(1)}, f32[16,672]{1,0:T(8,128)S(1)}, u32[]{:S(2)}, u32[]{:S(2)}) collective-permute-start(f32[16,672]{1,0:T(8,128)S(1)} %bitcast.20), channel_id=1, source_target_pairs={{0,1},{1,2},{2,3},{3,4},{4,5},{5,6},{6,7},{7,8},{8,9},{9,10},{10,1... | collective-permute-start | bytes 129032 | tf_op jit(solution)/shard_map/ppermute | solution.py:467
  176.3 0.7 compare_reduce_fusion
  177.0 1.3 collective-permute-start.3
  178.3 1.4 add_select_fusion
  179.7 1.5 scatter-add.6
  181.2 1.7 collective-permute-done.3
  182.9 0.9 slice_add_fusion
  183.8 1.5 scatter-add.9
  (30 shorter events, 0.5 us)
Async XLA Ops:
  0.0 7.2 %copy-start.6 = (s32[144,64]{0,1:T(8,128)S(1)}, s32[144,64]{0,1:T(8,128)}, u32[]{:S(2)}) copy-start(s32[144,64]{0,1:T(8,128)} %param.20) | copy-start | bytes 110596
  0.9 7.4 %collective-permute-start = (f32[16,672]{1,0:T(8,128)S(1)}, f32[16,672]{1,0:T(8,128)S(1)}, u32[]{:S(2)}, u32[]{:S(2)}) collective-permute-start(f32[16,672]{1,0:T(8,128)S(1)} %get-tuple-element.60), channel_id=1, source_target_pairs={{0,1},{1,2},{2,3},{3,4},{4,5},{5,6},{6,7},{7,8},{8,9},{9,10},{10,1... | collective-permute-start | bytes 129032 | tf_op jit(solution)/shard_map/ppermute | solution.py:467
  5.8 6.3 %copy-start = (f32[16,5376]{1,0:T(8,128)S(1)}, f32[16,5376]{1,0:T(8,128)}, u32[]{:S(2)}) copy-start(f32[16,5376]{1,0:T(8,128)} %res.1) | copy-start | bytes 1032196
  5.8 6.3 %collective-permute-start.1 = (f32[16,672]{1,0:T(8,128)S(1)}, f32[16,672]{1,0:T(8,128)S(1)}, u32[]{:S(2)}, u32[]{:S(2)}) collective-permute-start(f32[16,672]{1,0:T(8,128)S(1)} %get-tuple-element.59), channel_id=1, source_target_pairs={{1,0},{2,1},{3,2},{4,3},{5,4},{6,5},{7,6},{8,7},{9,8},{10,9},{11,1... | collective-permute-start | bytes 129032 | tf_op jit(solution)/shard_map/ppermute | solution.py:467
  7.3 0.7 copy-start.9
  7.4 0.7 copy-start.8
  7.4 0.8 copy-start.7
  8.2 3.9 %copy-start.1 = (f32[144,192]{1,0:T(8,128)S(1)}, f32[144,192]{1,0:T(8,128)}, u32[]{:S(2)}) copy-start(f32[144,192]{1,0:T(8,128)} %pi.1) | copy-start | bytes 331780
  8.4 3.7 %copy-start.2 = (f32[64,64]{1,0:T(8,128)S(1)}, f32[64,64]{1,0:T(8,128)}, u32[]{:S(2)}) copy-start(f32[64,64]{1,0:T(8,128)} %stiff.1) | copy-start | bytes 49156
  8.4 3.7 %copy-start.3 = (f32[64,64]{1,0:T(8,128)S(1)}, f32[64,64]{1,0:T(8,128)}, u32[]{:S(2)}) copy-start(f32[64,64]{1,0:T(8,128)} %mass.1) | copy-start | bytes 49156
  12.1 0.7 copy-start.4
  12.1 0.7 copy-start.5
  172.9 5.3 %collective-permute-start.2 = (f32[16,672]{1,0:T(8,128)S(1)}, f32[16,672]{1,0:T(8,128)S(1)}, u32[]{:S(2)}, u32[]{:S(2)}) collective-permute-start(f32[16,672]{1,0:T(8,128)S(1)} %bitcast.20), channel_id=1, source_target_pairs={{0,1},{1,2},{2,3},{3,4},{4,5},{5,6},{6,7},{7,8},{8,9},{9,10},{10,1... | collective-permute-start | bytes 129032 | tf_op jit(solution)/shard_map/ppermute | solution.py:467
  177.0 6.0 %collective-permute-start.3 = (f32[16,672]{1,0:T(8,128)S(1)}, f32[16,672]{1,0:T(8,128)S(1)}, u32[]{:S(2)}, u32[]{:S(2)}) collective-permute-start(f32[16,672]{1,0:T(8,128)S(1)} %bitcast.19), channel_id=1, source_target_pairs={{1,0},{2,1},{3,2},{4,3},{5,4},{6,5},{7,6},{8,7},{9,8},{10,9},{11,1... | collective-permute-start | bytes 129032 | tf_op jit(solution)/shard_map/ppermute | solution.py:467
where the time goes:
time: 186 us; the launch traced here: 185 us
  blocking collectives  100 us (54%)
  Pallas kernels  59.8 us (32%)
  starting transfers between devices  10.9 us (6%)
  local copies, waits for them, and re-layouts  5.63 us (3%)
  waiting for transfers between devices  5.42 us (3%)
  other arithmetic  3.1 us (2%)
    all_to_all x4, blocking collectives, exchange(): return lax.all_to_all(array, 'dev', split_axis=0, concat_axis=0, tiled=True)  100 us
    pallas_call x5, Pallas kernels, call(): pl.pallas_call(body, out_shape=[jax.ShapeDtypeStruct(*o) for o in outs],...  59.8 us
    ppermute x4, starting transfers between devices, shifted(): lax.ppermute(array, width_axes, pairs if up else [(j, i) for i, j in pairs])  10.9 us
    ppermute x4, waiting for transfers between devices, shifted(): lax.ppermute(array, width_axes, pairs if up else [(j, i) for i, j in pairs])  5.42 us
  transfers between devices with their start and end apart: 4, of which 2 were waited for; matrix products, arithmetic and copies ran while one was open for 2% of the time, Pallas kernels for 0%

commit v1 on v0

v1 whole, which is shorter than its diff:
```python
import functools
import jax
import jax.numpy as jnp
from jax import lax
from jax.experimental import pallas as pl
from jax.experimental.pallas import tpu as pltpu
from jax.sharding import PartitionSpec as P

N_LOC = 1728
CHUNK = 256
WIDE = 512
F32 = jnp.float32
BF16 = jnp.bfloat16
AUX = 8
CHEB_LOW = 0.3
CHEB_HIGH = 2.0
VMEM_BYTES = 50 * 1024 * 1024


def cheb_factors():
    center = 0.5 * (CHEB_HIGH + CHEB_LOW)
    half_width = 0.5 * (CHEB_HIGH - CHEB_LOW)
    sigma_ratio = center / half_width
    rho_first = 1.0 / sigma_ratio
    rho_second = 1.0 / (2.0 * sigma_ratio - rho_first)
    return (1.0 / center, 1.0 + rho_second * rho_first, 2.0 * rho_second / half_width)


def iota(shape, dim):
    return lax.broadcasted_iota(jnp.int32, shape, dim)


def dot(a, b):
    return lax.dot_general(a, b, (((1,), (0,)), ((), ())), preferred_element_type=F32)


def dot_nt(a, b):
    return lax.dot_general(a, b, (((1,), (1,)), ((), ())), preferred_element_type=F32)


def split(x):
    high = x.astype(BF16)
    low = (x - high.astype(F32)).astype(BF16)
    return high, low


def split_wide(x):
    high, low = split(x)
    return jnp.concatenate([high, low], axis=1)


def ones_where(mask):
    return jnp.where(mask, 1.0, 0.0).astype(BF16)


def onehot(low_index):
    return ones_where(iota((CHUNK, low_index.shape[1]), 0) == low_index)


def gather_cols(table2, high_index, hot, groups, rows):
    found = dot(table2, jnp.concatenate([hot, hot], axis=0))
    picked = jnp.zeros((rows, hot.shape[1]), F32)
    for h in range(groups):
        picked = jnp.where(high_index == h, found[h * rows : (h + 1) * rows], picked)
    return picked


def scatter_cols(values, high_index, hot, groups):
    high, low = split(values)
    high, low = high.astype(F32), low.astype(F32)
    masks = [high_index == h for h in range(groups)]
    high_rows = jnp.concatenate([jnp.where(m, high, 0.0) for m in masks], axis=0)
    low_rows = jnp.concatenate([jnp.where(m, low, 0.0) for m in masks], axis=0)
    both = jnp.concatenate([high_rows.astype(BF16), low_rows.astype(BF16)], axis=1)
    return dot_nt(both, jnp.concatenate([hot, hot], axis=1))


def dot3(x, w_high, w_low):
    high, low = split(x)
    return dot(high, w_high) + dot(low, w_high) + dot(high, w_low)


def dot3_nt(x, w_high, w_low):
    high, low = split(x)
    return dot_nt(high, w_high) + dot_nt(low, w_high) + dot_nt(high, w_low)


def block_weights(block, copies):
    size = block.shape[0]
    total = size * copies
    spread = ones_where(iota((size, total), 1) % size == iota((size, total), 0))
    keep = iota((total, total), 0) // size == iota((total, total), 1) // size
    out = []
    for part in split(block):
        row = dot(part, spread)
        full = jnp.concatenate([row] * copies, axis=0)
        out.append(jnp.where(keep, full, 0.0).astype(BF16))
    return out


def pi_weights(pi_rows, copies, nodes):
    count, total = pi_rows.shape
    comps = total // nodes
    width = comps * copies * nodes
    col, row = iota((total, width), 1), iota((total, width), 0)
    per = copies * nodes
    spread = ones_where((col // per == row // nodes) & (col % nodes == row % nodes))
    shape = (copies * count, width)
    keep = iota(shape, 0) // count == (iota(shape, 1) % per) // nodes
    out = []
    for part in split(pi_rows):
        one = dot(part, spread)
        full = jnp.concatenate([one] * copies, axis=0)
        out.append(jnp.where(keep, full, 0.0).astype(BF16))
    return out


def keep_parts(ref, parts):
    ref[0] = parts[0]
    ref[1] = parts[1]


def prepare_coefs(coef_ref, stiff_ref, mass_ref, coef_q, diag_q):
    nodes = stiff_ref.shape[0]
    eye = iota((nodes, nodes), 0) == iota((nodes, nodes), 1)
    sd = jnp.sum(jnp.where(eye, stiff_ref[...], 0.0), axis=0, keepdims=True)
    md = jnp.sum(jnp.where(eye, mass_ref[...], 0.0), axis=0, keepdims=True)
    diags = jnp.concatenate([sd, md, jnp.zeros((6, nodes), F32)], axis=0)
    d_parts = split(diags)
    c_parts = split(coef_ref[...])
    elems = coef_ref.shape[1]

    def body(i, _):
        lane = iota((elems, WIDE), 1) + i * WIDE
        by_elem = ones_where(lane // nodes == iota((elems, WIDE), 0))
        lane_n = iota((nodes, WIDE), 1)
        by_node = ones_where(lane_n % nodes == iota((nodes, WIDE), 0))
        coef = dot(c_parts[0], by_elem) + dot(c_parts[1], by_elem)
        diag = dot(d_parts[0], by_node) + dot(d_parts[1], by_node)
        at = pl.ds(pl.multiple_of(i * WIDE, WIDE), WIDE)
        coef_q[:, at] = coef
        base = coef[0:1] * diag[0:1]
        rows = iota((AUX, WIDE), 0)
        terms = jnp.zeros((AUX, WIDE), F32)
        for c in range(3):
            terms = jnp.where(rows == c, base + diag[1:2] * coef[1 + c : 2 + c], terms)
        diag_q[:, at] = terms
        return 0

    lax.fori_loop(0, coef_q.shape[1] // WIDE, body, 0)


def prepare_places(peers, owner_ref, slot_ref, local_ref, pos_hi, hot_el, slot_buf):
    touched = owner_ref.shape[1]
    capacity = 2 * touched // peers
    groups = 2 * touched // CHUNK
    tri = ones_where(iota((CHUNK, CHUNK), 0) < iota((CHUNK, CHUNK), 1))
    carry = jnp.zeros((peers, 1), F32)
    place = []
    for i in range(touched // CHUNK):
        own = owner_ref[:, i * CHUNK : (i + 1) * CHUNK]
        hot = jnp.where(iota((peers, CHUNK), 0) == own, 1.0, 0.0)
        before = dot(hot.astype(BF16), tri) + carry
        rank = jnp.sum(hot * before, axis=0, keepdims=True)
        carry = carry + jnp.sum(hot, axis=1, keepdims=True)
        place.append(own * capacity + rank.astype(jnp.int32))
    rows8 = iota((AUX, CHUNK), 0)
    table_hi = jnp.zeros((AUX, CHUNK), F32)
    table_lo = jnp.zeros((AUX, CHUNK), F32)
    slots = jnp.zeros((2 * groups, CHUNK), F32)
    for i, pos in enumerate(place):
        high, low = pos // CHUNK, pos % CHUNK
        table_hi = jnp.where(rows8 == i, high.astype(F32), table_hi)
        table_lo = jnp.where(rows8 == i, low.astype(F32), table_lo)
        slot = slot_ref[:, i * CHUNK : (i + 1) * CHUNK] + 1
        here = iota((groups, CHUNK), 0) == high
        s_hi = jnp.where(here, (slot // CHUNK).astype(F32), 0.0)
        s_lo = jnp.where(here, (slot % CHUNK).astype(F32), 0.0)
        both = jnp.concatenate([s_hi, s_lo], axis=0).astype(BF16)
        slots = slots + dot_nt(both, onehot(low))
    slot_buf[...] = slots[:groups] * float(CHUNK) + slots[groups:]
    table = jnp.concatenate([table_hi, table_lo], axis=0).astype(BF16)

    def body(i, _):
        at = pl.ds(pl.multiple_of(i * WIDE, WIDE), WIDE)
        local = local_ref[:, at]
        found = dot(table, onehot(local % CHUNK))
        here = iota((AUX, WIDE), 0) == local // CHUNK
        high = jnp.sum(jnp.where(here, found[:AUX], 0.0), axis=0, keepdims=True)
        low = jnp.sum(jnp.where(here, found[AUX:], 0.0), axis=0, keepdims=True)
        pos_hi[:, at] = high.astype(jnp.int32)
        hot_el[:, at] = onehot(low.astype(jnp.int32))
        return 0

    lax.fori_loop(0, local_ref.shape[1] // WIDE, body, 0)


def edge_gather(table2, emap_hi, hot_ed, groups, rhs, xa, xb):
    a_chunks = xa.shape[0] // rhs * CHUNK // WIDE

    def take(i):
        at = pl.ds(pl.multiple_of(i * WIDE, WIDE), WIDE)
        return gather_cols(table2[...], emap_hi[:, at], hot_ed[:, at], groups, rhs)

    def body(i, _):
        got = take(i)
        for s in range(2):
            at = pl.multiple_of((2 * i + s) * rhs, rhs)
            xa[pl.ds(at, rhs), :] = got[:, s * CHUNK : (s + 1) * CHUNK]
        return 0

    lax.fori_loop(0, a_chunks, body, 0)
    for i in range(2):
        got = take(a_chunks + i)
        for s in range(4):
            xb[(4 * i + s) * rhs : (4 * i + s + 1) * rhs, :] = got[:, s * 128 : (s + 1) * 128]


def restrict(xa, xb, wa, wb, rhs, terms):
    ya = dot3(xa[...], wa[0], wa[1])
    yb = dot3(xb[...], wb[0], wb[1])
    for p in range(xa.shape[0] // rhs):
        for c in range(3):
            first = ya[p * rhs : (p + 1) * rhs, c * 128 : (c + 1) * 128]
            lane = c * 512 + (p % 4) * 128
            second = yb[(p // 4) * rhs : (p // 4 + 1) * rhs, lane : lane + 128]
            terms[c * rhs : (c + 1) * rhs, p * 128 : (p + 1) * 128] = first + second


def scatter_elems(terms, pos_hi, hot_el, acc):
    rows, total = terms.shape
    groups = acc.shape[0] // rows
    acc[...] = jnp.zeros_like(acc)

    def body(i, _):
        at = pl.ds(pl.multiple_of(i * WIDE, WIDE), WIDE)
        acc[...] += scatter_cols(terms[:, at], pos_hi[:, at], hot_el[:, at], groups)
        return 0

    lax.fori_loop(0, total // WIDE, body, 0)


def lay_out(send, acc, rows, first_row):
    capacity = send.shape[2]
    for h in range(acc.shape[0] // rows):
        step = min(capacity, CHUNK)
        for s in range(CHUNK // step):
            lane = h * CHUNK + s * step
            peer, off = lane // capacity, lane % capacity
            send[peer, first_row : first_row + rows, off : off + step] = acc[
                h * rows : (h + 1) * rows, s * step : (s + 1) * step
            ]


def table_from(got, rows, table, table2):
    peers, _, capacity = got.shape
    for h in range(peers * capacity // CHUNK):
        step = min(capacity, CHUNK)
        parts = []
        for s in range(CHUNK // step):
            lane = h * CHUNK + s * step
            peer, off = lane // capacity, lane % capacity
            parts.append(got[peer, :rows, off : off + step])
        value = parts[0] if len(parts) == 1 else jnp.concatenate(parts, axis=1)
        table[h * rows : (h + 1) * rows, :] = value
    table2[...] = split_wide(table[...])


def gather_elems(table2, pos_hi, hot_el, rows, visit):
    groups = table2.shape[0] // rows

    def body(i, _):
        at = pl.ds(pl.multiple_of(i * WIDE, WIDE), WIDE)
        visit(i, gather_cols(table2[...], pos_hi[:, at], hot_el[:, at], groups, rows))
        return 0

    lax.fori_loop(0, pos_hi.shape[1] // WIDE, body, 0)


def home_index(slot_row):
    slot = slot_row.astype(jnp.int32) - 1
    return jnp.where(slot < 0, -1, slot // CHUNK), jnp.maximum(slot, 0) % CHUNK


def apply_operator(x_all, ws, wm, coef_q, rhs, terms):
    rows = 3 * rhs
    stiff = dot3(x_all[...], ws[0], ws[1])
    mass = dot3(x_all[...], wm[0], wm[1])
    tensor = ((1, 4, 5), (4, 2, 6), (5, 6, 3))
    for i in range(x_all.shape[0] // rows):
        lanes = slice(i * CHUNK, (i + 1) * CHUNK)
        coef = coef_q[:, lanes]
        for c in range(3):
            at = i * rows + c * rhs
            total = coef[0:1] * stiff[at : at + rhs]
            for c2 in range(3):
                t = tensor[c][c2]
                at2 = i * rows + c2 * rhs
                total = total + coef[t : t + 1] * mass[at2 : at2 + rhs]
            terms[c * rhs : (c + 1) * rhs, lanes] = total


def edge_scatter(ea, eb, emap_hi, hot_ed, rhs, acc):
    groups = acc.shape[0] // rhs
    a_chunks = ea.shape[0] // rhs * CHUNK // WIDE
    acc[...] = jnp.zeros_like(acc)

    def put(i, values):
        at = pl.ds(pl.multiple_of(i * WIDE, WIDE), WIDE)
        acc[...] += scatter_cols(values, emap_hi[:, at], hot_ed[:, at], groups)

    def body(i, _):
        parts = [ea[pl.ds(pl.multiple_of((2 * i + s) * rhs, rhs), rhs), :] for s in range(2)]
        put(i, jnp.concatenate(parts, axis=1))
        return 0

    lax.fori_loop(0, a_chunks, body, 0)
    for i in range(2):
        parts = [eb[(4 * i + s) * rhs : (4 * i + s + 1) * rhs, :] for s in range(4)]
        put(a_chunks + i, jnp.concatenate(parts, axis=1))


def kernel(
    grps, peers, home, e_groups,
    res, emap, local, owner, slot, coef, pi, stiff, mass,
    out,
    rim_in, rim_out, rim_back, aux_send, aux_recv, send, recv,
    hot_el, hot_ed, hot_home, emap_hi, pos_hi, home_hi, slot_buf, coef_q, diag_q,
    wa, wb, ws, wm, e_table, e_table2, xa, xb, x3a, x3b, ea, eb, terms,
    n_table, n_table2, x_all, acc, acc_d, h_table, h_table2, rhs_nodes, h_acc, floored, e_acc,
    rim_s, rim_r, aux_s, aux_r, x_s, x_r, back_s, back_r,
):
    grp, me = lax.axis_index("grp"), lax.axis_index("dev")
    rhs = res.shape[0] // 2
    rows = 3 * rhs
    edges = res.shape[1]
    width = rim_in.shape[2]
    first, keep, step = cheb_factors()
    up, down = me + 1, me + peers - 1
    after_id = (lax.rem(grp + up // peers, grps), lax.rem(up, peers))
    before_id = (lax.rem(grp + grps - 1 + down // peers, grps), lax.rem(down, peers))

    def remote(src, dst, ssem, rsem, device):
        return pltpu.make_async_remote_copy(
            src_ref=src,
            dst_ref=dst,
            send_sem=ssem,
            recv_sem=rsem,
            device_id=device,
            device_id_type=pl.DeviceIdType.MESH,
        )

    def to_peer(src, dst, ssem, rsem, d):
        peer = lax.rem(me + d, peers)
        return remote(src.at[peer], dst.at[me], ssem.at[d], rsem.at[me], (grp, peer))

    def each_peer(do):
        def body(d, _):
            do(d)
            return 0

        lax.fori_loop(1, peers, body, 0)

    def wait_from(src, dst, ssem, rsem, s):
        remote(src.at[s], dst.at[s], ssem.at[0], rsem.at[s], (grp, s)).wait_recv()

    def source(d):
        return lax.rem(me + peers - d, peers)

    def refs(stage, half):
        return (send.at[stage, half], recv.at[stage, half], x_s.at[stage, half], x_r.at[stage, half])

    barrier = pltpu.get_barrier_semaphore()

    def greet(d):
        pl.semaphore_signal(
            barrier, 1, device_id=(grp, lax.rem(me + d, peers)),
            device_id_type=pl.DeviceIdType.MESH,
        )

    each_peer(greet)
    for device in (before_id, after_id):
        pl.semaphore_signal(barrier, 1, device_id=device, device_id_type=pl.DeviceIdType.MESH)
    pl.semaphore_wait(barrier, peers + 1)

    rims = [
        remote(res.at[:, edges - width :], rim_in.at[0], rim_s.at[0], rim_r.at[0], after_id),
        remote(res.at[:, :width], rim_in.at[1], rim_s.at[1], rim_r.at[1], before_id),
    ]
    for copy in rims:
        copy.start()

    prepare_places(peers, owner, slot, local, pos_hi, hot_el, slot_buf)
    prepare_coefs(coef, stiff, mass, coef_q, diag_q)
    scatter_elems(diag_q, pos_hi, hot_el, acc_d)
    for g in range(slot_buf.shape[0]):
        acc_d[g * AUX + 3 : g * AUX + 4, :] = slot_buf[g : g + 1, :]
    lay_out(aux_send, acc_d, AUX, 0)
    each_peer(lambda d: to_peer(aux_send, aux_recv, aux_s, aux_r, d).start())

    keep_parts(wa, pi_weights(pi[:128], 2, stiff.shape[0]))
    keep_parts(wb, pi_weights(pi[128:], 8, stiff.shape[0]))
    index = emap[...]
    emap_hi[...] = index // CHUNK

    def hot_edges(i, _):
        at = pl.ds(pl.multiple_of(i * WIDE, WIDE), WIDE)
        hot_ed[:, at] = onehot(emap[:, at] % CHUNK)
        return 0

    lax.fori_loop(0, emap.shape[1] // WIDE, hot_edges, 0)
    for copy in rims:
        copy.wait_recv()

    def restrict_half(half):
        mine = slice(half * rhs, (half + 1) * rhs)
        e_table[...] = jnp.zeros_like(e_table)
        blocks = [res[mine, i * CHUNK : (i + 1) * CHUNK] for i in range(edges // CHUNK)]
        for side in range(2):
            for i in range(width // CHUNK):
                blocks.append(rim_in[side, mine, i * CHUNK : (i + 1) * CHUNK])
        for h, block in enumerate(blocks):
            e_table[h * rhs : (h + 1) * rhs, :] = block
        e_table2[...] = split_wide(e_table[...])
        edge_gather(e_table2, emap_hi, hot_ed, e_groups, rhs, xa, xb)
        restrict(xa, xb, wa, wb, rhs, terms)
        scatter_elems(terms, pos_hi, hot_el, acc)
        lay_out(send.at[0, half], acc, rows, 0)
        each_peer(lambda d: to_peer(*refs(0, half), d).start())

    def learn_home():
        floored[...] = jnp.zeros_like(floored)

        def learn(got, s):
            high, low = home_index(got[s, 3:4, :])
            hot = onehot(low)
            home_hi[s] = high
            hot_home[s] = hot
            floored[...] += scatter_cols(got[s], high, hot, home)

        def other(d):
            s = source(d)
            wait_from(aux_send, aux_recv, aux_s, aux_r, s)
            learn(aux_recv, s)

        learn(aux_send, me)
        each_peer(other)
        floored[...] = jnp.maximum(floored[...], 1.0)

    def home_sum(stage, half, total):
        src, dst, ssem, rsem = refs(stage, half)
        total[...] = scatter_cols(src[me], home_hi[me], hot_home[me], home)

        def other(d):
            s = source(d)
            wait_from(src, dst, ssem, rsem, s)
            total[...] += scatter_cols(dst[s], home_hi[s], hot_home[s], home)

        each_peer(other)

    def home_values(h, c, half, second):
        at = slice(h * rows + c * rhs, h * rows + (c + 1) * rhs)
        weight = floored[h * AUX + c : h * AUX + c + 1, :]
        nodes = rhs_nodes[half, at, :]
        value = first * nodes / weight
        if second:
            value = keep * value + step * (nodes - h_acc[at, :]) / weight
        h_table[at, :] = value

    def home_half(stage, half, second):
        home_sum(stage, half, h_acc if second else rhs_nodes.at[half])
        h_table[...] = jnp.zeros_like(h_table)
        for h in range(home):
            for c in range(3):
                home_values(h, c, half, second)
        h_table2[...] = split_wide(h_table[...])
        src, dst, ssem, rsem = refs(stage + 1, half)

        def reply(d):
            peer = lax.rem(me + d, peers)
            src[peer] = gather_cols(h_table2[...], home_hi[peer], hot_home[peer], home, rows)
            to_peer(src, dst, ssem, rsem, d).start()

        each_peer(reply)
        dst[me] = gather_cols(h_table2[...], home_hi[me], hot_home[me], home, rows)

    def fetched(stage, half):
        each_peer(lambda d: wait_from(*refs(stage, half), source(d)))
        table_from(recv.at[stage, half], rows, n_table, n_table2)

    def operate_half(half):
        fetched(1, half)

        def visit(i, value):
            for s in range(2):
                at = pl.multiple_of((2 * i + s) * rows, rows)
                x_all[pl.ds(at, rows), :] = value[:, s * CHUNK : (s + 1) * CHUNK]

        gather_elems(n_table2, pos_hi, hot_el, rows, visit)
        apply_operator(x_all, ws, wm, coef_q, rhs, terms)
        scatter_elems(terms, pos_hi, hot_el, acc)
        lay_out(send.at[2, half], acc, rows, 0)
        each_peer(lambda d: to_peer(*refs(2, half), d).start())

    def backs(half):
        return [
            remote(
                rim_out.at[half, 0], rim_back.at[half, 1], back_s.at[half, 0],
                back_r.at[half, 0], before_id,
            ),
            remote(
                rim_out.at[half, 1], rim_back.at[half, 0], back_s.at[half, 1],
                back_r.at[half, 1], after_id,
            ),
        ]

    def prolong_half(half):
        fetched(3, half)

        def visit(i, value):
            for c in range(3):
                part = value[c * rhs : (c + 1) * rhs]
                x3b[pl.ds(pl.multiple_of(i * rhs, rhs), rhs), c * WIDE : (c + 1) * WIDE] = part
                for s in range(4):
                    at = pl.multiple_of((4 * i + s) * rhs, rhs)
                    x3a[pl.ds(at, rhs), c * 128 : (c + 1) * 128] = part[:, s * 128 : (s + 1) * 128]

        gather_elems(n_table2, pos_hi, hot_el, rows, visit)
        ea[...] = dot3_nt(x3a[...], wa[0], wa[1])
        eb[...] = dot3_nt(x3b[...], wb[0], wb[1])
        edge_scatter(ea, eb, emap_hi, hot_ed, rhs, e_acc.at[half])
        h = edges // CHUNK
        for side in range(2):
            for i in range(width // CHUNK):
                rim_out[half, side, :, i * CHUNK : (i + 1) * CHUNK] = e_acc[
                    half, h * rhs : (h + 1) * rhs, :
                ]
                h += 1
        for copy in backs(half):
            copy.start()

    restrict_half(0)
    learn_home()
    restrict_half(1)
    home_half(0, 0, False)
    keep_parts(ws, block_weights(stiff[...], 4))
    keep_parts(wm, block_weights(mass[...], 4))
    home_half(0, 1, False)
    operate_half(0)
    operate_half(1)
    home_half(2, 0, True)
    home_half(2, 1, True)
    prolong_half(0)
    prolong_half(1)

    count, reach = edges // CHUNK, width // CHUNK
    for half in range(2):
        mine = slice(half * rhs, (half + 1) * rhs)
        for copy in backs(half):
            copy.wait_recv()
        for h in range(count):
            value = e_acc[half, h * rhs : (h + 1) * rhs, :]
            if h < reach:
                value = value + rim_back[half, 0, :, h * CHUNK : (h + 1) * CHUNK]
            if h >= count - reach:
                at = (h - count + reach) * CHUNK
                value = value + rim_back[half, 1, :, at : at + CHUNK]
            out[mine, h * CHUNK : (h + 1) * CHUNK] = value

    for copy in rims + backs(0) + backs(1):
        copy.wait_send()

    def sent(d):
        to_peer(aux_send, aux_recv, aux_s, aux_r, d).wait_send()
        for stage in range(4):
            for half in range(2):
                to_peer(*refs(stage, half), d).wait_send()

    each_peer(sent)


def per_device(
    residual, pi, stiff, mass, permittivity, curl, edge_map, local_map, node_owner, node_slot
):
    rhs, edges = residual.shape
    ed, elems = edge_map.shape
    nodes = local_map.shape[0]
    touched = node_owner.shape[0]
    peers, grps = lax.axis_size("dev"), lax.axis_size("grp")
    capacity = 2 * touched // peers
    rim = edges // 8
    width = -(-rim // CHUNK) * CHUNK
    entries = nodes * elems
    place = edge_map.T - rim
    place = jnp.where(
        place < 0,
        place + edges + width,
        jnp.where(place >= edges, place + width, place),
    )
    emap = jnp.concatenate([place[:, :128].reshape(1, -1), place[:, 128:].reshape(1, -1)], axis=1)
    local = local_map.T.reshape(1, -1)
    coef = jnp.concatenate([curl[None], permittivity, jnp.zeros((1, elems), F32)], axis=0)
    groups = 2 * touched // CHUNK
    home = -(-N_LOC // CHUNK)
    home_even = home + home % 2
    e_groups = (edges + 2 * width) // CHUNK
    e_even = e_groups + e_groups % 2
    pairs, eights = elems // 2, elems // 8
    half = rhs // 2
    rows = 3 * half
    scratch = [
        ((2, rhs, width), F32),
        ((2, 2, half, width), F32),
        ((2, 2, half, width), F32),
        ((peers, AUX, capacity), F32),
        ((peers, AUX, capacity), F32),
        ((4, 2, peers, rows, capacity), F32),
        ((4, 2, peers, rows, capacity), F32),
        ((CHUNK, entries), BF16),
        ((CHUNK, ed * elems), BF16),
        ((peers, CHUNK, capacity), BF16),
        ((1, ed * elems), jnp.int32),
        ((1, entries), jnp.int32),
        ((peers, 1, capacity), jnp.int32),
        ((groups, CHUNK), F32),
        ((AUX, entries), F32),
        ((AUX, entries), F32),
        ((2, 256, 384), BF16),
        ((2, 128, 1536), BF16),
        ((2, CHUNK, CHUNK), BF16),
        ((2, CHUNK, CHUNK), BF16),
        ((e_even * half, CHUNK), F32),
        ((e_even * half, 2 * CHUNK), BF16),
        ((pairs * half, 256), F32),
        ((eights * half, 128), F32),
        ((pairs * half, 384), F32),
        ((eights * half, 1536), F32),
        ((pairs * half, 256), F32),
        ((eights * half, 128), F32),
        ((rows, entries), F32),
        ((groups * rows, CHUNK), F32),
        ((groups * rows, 2 * CHUNK), BF16),
        ((entries // CHUNK * rows, CHUNK), F32),
        ((groups * rows, CHUNK), F32),
        ((groups * AUX, CHUNK), F32),
        ((home_even * rows, CHUNK), F32),
        ((home_even * rows, 2 * CHUNK), BF16),
        ((2, home * rows, CHUNK), F32),
        ((home * rows, CHUNK), F32),
        ((home * AUX, CHUNK), F32),
        ((2, e_groups * half, CHUNK), F32),
    ]
    sems = [(2,), (2,), (peers,), (peers,), (4, 2, peers), (4, 2, peers), (2, 2), (2, 2)]
    vmem = pl.BlockSpec(memory_space=pltpu.VMEM)
    return pl.pallas_call(
        functools.partial(kernel, grps, peers, home, e_groups),
        out_shape=jax.ShapeDtypeStruct((rhs, edges), F32),
        in_specs=[vmem] * 9,
        out_specs=vmem,
        scratch_shapes=[pltpu.VMEM(*s) for s in scratch]
        + [pltpu.SemaphoreType.DMA(s) for s in sems],
        compiler_params=pltpu.CompilerParams(
            collective_id=0, has_side_effects=True, vmem_limit_bytes=VMEM_BYTES
        ),
    )(residual, emap, local, node_owner[None], node_slot[None], coef, pi, stiff, mass)


def solution(mesh):
    both = ("grp", "dev")
    in_specs = (
        P(None, both), P(), P(), P(), P(None, both), P(both), P(None, both), P(None, both),
        P(both), P(both),
    )
    return jax.shard_map(
        per_device, mesh=mesh, in_specs=in_specs, out_specs=P(None, both), check_vma=False
    )
```

time: 186 us -> 127 us (0.68)
  blocking collectives: 100 us -> 0 us
  Pallas kernels: 59.8 us -> 120 us
  starting transfers between devices: 10.9 us -> 0 us
  waiting for transfers between devices: 5.42 us -> 0 us
    all_to_all x4 -> x0, blocking collectives: 100 us -> none  [exchange(): return lax.all_to_all(array, 'dev', split_axis=0, concat_axis=0, tiled=True)]
    pallas_call x5 -> x1, Pallas kernels: 59.8 us -> 120 us  [per_device(): pl.pallas_call(functools.partial(kernel, grps, peers, home, e_groups), ou...]
    ppermute x4 -> x0, starting transfers between devices: 10.9 us -> none  [shifted(): lax.ppermute(array, width_axes, pairs if up else [(j, i) for i, j in pairs])]
    ppermute x4 -> x0, waiting for transfers between devices: 5.42 us -> none  [shifted(): lax.ppermute(array, width_axes, pairs if up else [(j, i) for i, j in pairs])]
    scatter-add x2 -> x0, local copies, waits for them, and re-layouts: 3.05 us -> none  [the longest x1 1.53 us: per_device(): return own.at[:, edges - rim:].add(from_after)]
    another operation x2 -> x0, other arithmetic: 2.13 us -> none
  transfers between devices with their start and end apart: 4 -> 0, of which waited for: 2 -> 0; matrix products, arithmetic and copies ran while one was open for 2% -> 0% of each run, Pallas kernels for 0% -> 0%
where the time goes in v1:
time: 127 us; the launch traced here: 126 us
  Pallas kernels  120 us (94%)
  local copies, waits for them, and re-layouts  4.11 us (3%)
  other arithmetic  1.66 us (1%)
    pallas_call x1, Pallas kernels, per_device(): pl.pallas_call(functools.partial(kernel, grps, peers, home, e_groups), ou...  120 us
    unnamed x13, local copies, waits for them, and re-layouts  3.02 us

profile of v1, /device:TPU:0, one launch (start us, length us, event | category | flops | bytes accessed | tf_op | source)
XLA Modules:
  0.0 126.3 jit_solution(16416481383530710576)
XLA Ops:
  0.0 0.0 copy-start
  0.0 0.1 pad.2.clone
  0.1 0.8 maximum_maximum_fusion.coef
  0.9 0.8 copy.12
  1.7 0.1 reshape.11.local
  1.8 0.9 fusion
  2.7 0.0 copy-start.1
  2.7 0.1 reshape.10
  2.8 0.0 copy-start.4
  2.8 0.0 copy-start.5
  2.8 0.0 copy-done
  2.8 0.8 copy-done.1
  3.6 0.0 copy-done.4
  3.6 0.0 copy-done.5
  3.6 0.0 copy-start.2
  3.6 0.8 copy-done.2
  4.3 0.0 copy-start.3
  4.3 0.8 copy-done.3
  5.1 120.5 %shard_map.100 = f32[16,5376]{1,0:T(8,128)S(1)} custom-call(f32[16,5376]{1,0:T(8,128)S(1)} %copy-done, s32[1,9216]{1,0:T(1,128)S(1)} %pad_add_fusion.emap, s32[1,4096]{1,0:T(1,128)S(1)} %reshape.11.local, s32[1,2048]{1,0:T(1,128)S(1)} %bitcast.15, s32[1,2048]{1,0:T(1,128)S(1)} %bitcast.16, f32[8,64]{1,0:T(8,128)S(1)} %maximum_maximum_fusion.coef, ...), custom_call_target="tpu_custom_call" | custom-call | tf_op jit(solution)/shard_map/pallas_call | solution.py:655
  125.6 0.7 copy.14
  (3 shorter events, 0.0 us)
Async XLA Ops:
  0.0 2.8 %copy-start = (f32[16,5376]{1,0:T(8,128)S(1)}, f32[16,5376]{1,0:T(8,128)}, u32[]{:S(2)}) copy-start(f32[16,5376]{1,0:T(8,128)} %res.1) | copy-start | bytes 1032196
  2.7 0.9 copy-start.1
  2.8 0.8 copy-start.4
  2.8 0.8 copy-start.5
  3.6 0.8 copy-start.2
  4.3 0.8 copy-start.3

commit v2 on v1

--- a/solution.py
+++ b/solution.py
@@ -14,7 +14,7 @@
 AUX = 8
 CHEB_LOW = 0.3
 CHEB_HIGH = 2.0
-VMEM_BYTES = 50 * 1024 * 1024
+VMEM_BYTES = 60 * 1024 * 1024
 
 
 def cheb_factors():
@@ -66,13 +66,25 @@
 
 
 def scatter_cols(values, high_index, hot, groups):
-    high, low = split(values)
-    high, low = high.astype(F32), low.astype(F32)
-    masks = [high_index == h for h in range(groups)]
-    high_rows = jnp.concatenate([jnp.where(m, high, 0.0) for m in masks], axis=0)
-    low_rows = jnp.concatenate([jnp.where(m, low, 0.0) for m in masks], axis=0)
-    both = jnp.concatenate([high_rows.astype(BF16), low_rows.astype(BF16)], axis=1)
-    return dot_nt(both, jnp.concatenate([hot, hot], axis=1))
+    count = 2 * values.shape[0] // 16
+    high = values.astype(BF16).astype(F32)
+    both = jnp.concatenate([high, values - high], axis=0).astype(BF16)
+    index = jnp.concatenate([high_index] * count, axis=0) if count > 1 else high_index
+    zero = jnp.zeros_like(both)
+    spread = [jnp.where(index == jnp.int16(h), both, zero) for h in range(groups)]
+    return dot_nt(jnp.concatenate(spread, axis=0), hot)
+
+
+def add_parts(acc, found, rows, fresh=False):
+    for h in range(found.shape[0] // (2 * rows)):
+        at = slice(h * rows, (h + 1) * rows)
+        low = 2 * h * rows
+        value = found[low : low + rows] + found[low + rows : low + 2 * rows]
+        acc[at, :] = value if fresh else acc[at, :] + value
+
+
+def wide16(index):
+    return jnp.broadcast_to(index, (16, index.shape[1])).astype(jnp.int16)
 
 
 def dot3(x, w_high, w_low):
@@ -150,7 +162,7 @@
     lax.fori_loop(0, coef_q.shape[1] // WIDE, body, 0)
 
 
-def prepare_places(peers, owner_ref, slot_ref, local_ref, pos_hi, hot_el, slot_buf):
+def prepare_places(peers, owner_ref, slot_ref, local_ref, pos_hi, pos_hi16, hot_el, slot_buf):
     touched = owner_ref.shape[1]
     capacity = 2 * touched // peers
     groups = 2 * touched // CHUNK
@@ -189,6 +201,7 @@
         high = jnp.sum(jnp.where(here, found[:AUX], 0.0), axis=0, keepdims=True)
         low = jnp.sum(jnp.where(here, found[AUX:], 0.0), axis=0, keepdims=True)
         pos_hi[:, at] = high.astype(jnp.int32)
+        pos_hi16[:, at] = wide16(high.astype(jnp.int32))
         hot_el[:, at] = onehot(low.astype(jnp.int32))
         return 0
 
@@ -227,28 +240,28 @@
             terms[c * rhs : (c + 1) * rhs, p * 128 : (p + 1) * 128] = first + second
 
 
-def scatter_elems(terms, pos_hi, hot_el, acc):
+def scatter_elems(terms, pos_hi16, hot_el, acc):
     rows, total = terms.shape
     groups = acc.shape[0] // rows
     acc[...] = jnp.zeros_like(acc)
 
     def body(i, _):
         at = pl.ds(pl.multiple_of(i * WIDE, WIDE), WIDE)
-        acc[...] += scatter_cols(terms[:, at], pos_hi[:, at], hot_el[:, at], groups)
+        add_parts(acc, scatter_cols(terms[:, at], pos_hi16[:, at], hot_el[:, at], groups), rows)
         return 0
 
     lax.fori_loop(0, total // WIDE, body, 0)
 
 
-def lay_out(send, acc, rows, first_row):
-    capacity = send.shape[2]
+def lay_out(send, acc, rows):
+    _, kept, capacity = send.shape
     for h in range(acc.shape[0] // rows):
         step = min(capacity, CHUNK)
         for s in range(CHUNK // step):
             lane = h * CHUNK + s * step
             peer, off = lane // capacity, lane % capacity
-            send[peer, first_row : first_row + rows, off : off + step] = acc[
-                h * rows : (h + 1) * rows, s * step : (s + 1) * step
+            send[peer, :, off : off + step] = acc[
+                h * rows : h * rows + kept, s * step : (s + 1) * step
             ]
 
 
@@ -300,14 +313,14 @@
             terms[c * rhs : (c + 1) * rhs, lanes] = total
 
 
-def edge_scatter(ea, eb, emap_hi, hot_ed, rhs, acc):
+def edge_scatter(ea, eb, emap_hi16, hot_ed, rhs, acc):
     groups = acc.shape[0] // rhs
     a_chunks = ea.shape[0] // rhs * CHUNK // WIDE
     acc[...] = jnp.zeros_like(acc)
 
     def put(i, values):
         at = pl.ds(pl.multiple_of(i * WIDE, WIDE), WIDE)
-        acc[...] += scatter_cols(values, emap_hi[:, at], hot_ed[:, at], groups)
+        add_parts(acc, scatter_cols(values, emap_hi16[:, at], hot_ed[:, at], groups), rhs)
 
     def body(i, _):
         parts = [ea[pl.ds(pl.multiple_of((2 * i + s) * rhs, rhs), rhs), :] for s in range(2)]
@@ -322,13 +335,15 @@
 
 def kernel(
     grps, peers, home, e_groups,
-    res, emap, local, owner, slot, coef, pi, stiff, mass,
+    res_in, emap, local, owner_in, slot_in, coef, pi_in, stiff_in, mass_in,
     out,
+    res, owner, slot, pi, stiff, mass,
     rim_in, rim_out, rim_back, aux_send, aux_recv, send, recv,
-    hot_el, hot_ed, hot_home, emap_hi, pos_hi, home_hi, slot_buf, coef_q, diag_q,
+    hot_el, hot_ed, hot_home, emap_hi, pos_hi, home_hi,
+    emap_hi16, pos_hi16, home_hi16, slot_buf, coef_q, diag_q,
     wa, wb, ws, wm, e_table, e_table2, xa, xb, x3a, x3b, ea, eb, terms,
     n_table, n_table2, x_all, acc, acc_d, h_table, h_table2, rhs_nodes, h_acc, floored, e_acc,
-    rim_s, rim_r, aux_s, aux_r, x_s, x_r, back_s, back_r,
+    rim_s, rim_r, aux_s, aux_r, x_s, x_r, back_s, back_r, in_s,
 ):
     grp, me = lax.axis_index("grp"), lax.axis_index("dev")
     rhs = res.shape[0] // 2
@@ -350,31 +365,46 @@
             device_id_type=pl.DeviceIdType.MESH,
         )
 
-    def to_peer(src, dst, ssem, rsem, d):
-        peer = lax.rem(me + d, peers)
-        return remote(src.at[peer], dst.at[me], ssem.at[d], rsem.at[me], (grp, peer))
+    def partner(m):
+        total, bit = me * 0, 1
+        while bit < peers:
+            total = total + bit * lax.rem(me // bit + m // bit, 2)
+            bit *= 2
+        return total
+
+    def to_peer(src, dst, ssem, rsem, m):
+        peer = partner(m)
+        return remote(src.at[peer], dst.at[me], ssem.at[m], rsem.at[m], (grp, peer))
 
     def each_peer(do):
-        def body(d, _):
-            do(d)
+        def body(i, _):
+            do(peers - 1 - i)
             return 0
 
-        lax.fori_loop(1, peers, body, 0)
-
-    def wait_from(src, dst, ssem, rsem, s):
-        remote(src.at[s], dst.at[s], ssem.at[0], rsem.at[s], (grp, s)).wait_recv()
-
-    def source(d):
-        return lax.rem(me + peers - d, peers)
+        lax.fori_loop(0, peers - 1, body, 0)
+
+    def wait_from(src, dst, ssem, rsem, m):
+        s = partner(m)
+        remote(src.at[s], dst.at[s], ssem.at[m], rsem.at[m], (grp, s)).wait_recv()
+        return s
 
     def refs(stage, half):
         return (send.at[stage, half], recv.at[stage, half], x_s.at[stage, half], x_r.at[stage, half])
 
+    loads = [
+        pltpu.make_async_copy(*pair, in_s.at[i])
+        for i, pair in enumerate(
+            [(owner_in, owner), (slot_in, slot), (pi_in, pi), (res_in, res), (stiff_in, stiff),
+             (mass_in, mass)]
+        )
+    ]
+    for load in loads:
+        load.start()
     barrier = pltpu.get_barrier_semaphore()
 
     def greet(d):
         pl.semaphore_signal(
-            barrier, 1, device_id=(grp, lax.rem(me + d, peers)),
+            barrier, 1, device_id=(grp, partner(d)),
             device_id_type=pl.DeviceIdType.MESH,
         )
 
@@ -384,33 +414,42 @@
     pl.semaphore_wait(barrier, peers + 1)
 
     rims = [
-        remote(res.at[:, edges - width :], rim_in.at[0], rim_s.at[0], rim_r.at[0], after_id),
-        remote(res.at[:, :width], rim_in.at[1], rim_s.at[1], rim_r.at[1], before_id),
+        remote(res_in.at[:, edges - width :], rim_in.at[0], rim_s.at[0], rim_r.at[0], after_id),
+        remote(res_in.at[:, :width], rim_in.at[1], rim_s.at[1], rim_r.at[1], before_id),
     ]
     for copy in rims:
         copy.start()
 
-    prepare_places(peers, owner, slot, local, pos_hi, hot_el, slot_buf)
-    prepare_coefs(coef, stiff, mass, coef_q, diag_q)
-    scatter_elems(diag_q, pos_hi, hot_el, acc_d)
-    for g in range(slot_buf.shape[0]):
-        acc_d[g * AUX + 3 : g * AUX + 4, :] = slot_buf[g : g + 1, :]
-    lay_out(aux_send, acc_d, AUX, 0)
-    each_peer(lambda d: to_peer(aux_send, aux_recv, aux_s, aux_r, d).start())
-
-    keep_parts(wa, pi_weights(pi[:128], 2, stiff.shape[0]))
-    keep_parts(wb, pi_weights(pi[128:], 8, stiff.shape[0]))
-    index = emap[...]
-    emap_hi[...] = index // CHUNK
+    loads[0].wait()
+    loads[1].wait()
+    prepare_places(peers, owner, slot, local, pos_hi, pos_hi16, hot_el, slot_buf)
+    loads[2].wait()
+    nodes = stiff.shape[0]
+    keep_parts(wa, pi_weights(pi[:128], 2, nodes))
+    keep_parts(wb, pi_weights(pi[128:], 8, nodes))
 
     def hot_edges(i, _):
         at = pl.ds(pl.multiple_of(i * WIDE, WIDE), WIDE)
-        hot_ed[:, at] = onehot(emap[:, at] % CHUNK)
+        index = emap[:, at]
+        emap_hi[:, at] = index // CHUNK
+        emap_hi16[:, at] = wide16(index // CHUNK)
+        hot_ed[:, at] = onehot(index % CHUNK)
         return 0
 
     lax.fori_loop(0, emap.shape[1] // WIDE, hot_edges, 0)
+    loads[3].wait()
     for copy in rims:
         copy.wait_recv()
+
+    def send_aux():
+        loads[4].wait()
+        loads[5].wait()
+        prepare_coefs(coef, stiff, mass, coef_q, diag_q)
+        scatter_elems(diag_q, pos_hi16, hot_el, acc_d)
+        for g in range(slot_buf.shape[0]):
+            acc_d[g * AUX + 3 : g * AUX + 4, :] = slot_buf[g : g + 1, :]
+        lay_out(aux_send, acc_d, AUX)
+        each_peer(lambda d: to_peer(aux_send, aux_recv, aux_s, aux_r, d).start())
 
     def restrict_half(half):
         mine = slice(half * rhs, (half + 1) * rhs)
@@ -424,8 +463,8 @@
         e_table2[...] = split_wide(e_table[...])
         edge_gather(e_table2, emap_hi, hot_ed, e_groups, rhs, xa, xb)
         restrict(xa, xb, wa, wb, rhs, terms)
-        scatter_elems(terms, pos_hi, hot_el, acc)
-        lay_out(send.at[0, half], acc, rows, 0)
+        scatter_elems(terms, pos_hi16, hot_el, acc)
+        lay_out(send.at[0, half], acc, rows)
         each_peer(lambda d: to_peer(*refs(0, half), d).start())
 
     def learn_home():
@@ -436,12 +475,13 @@
             hot = onehot(low)
             home_hi[s] = high
             hot_home[s] = hot
-            floored[...] += scatter_cols(got[s], high, hot, home)
+            high16 = wide16(high)
+            home_hi16[s] = high16
+            values = jnp.concatenate([got[s], jnp.zeros_like(got[s])], axis=0)
+            add_parts(floored, scatter_cols(values, high16, hot, home), AUX)
 
         def other(d):
-            s = source(d)
-            wait_from(aux_send, aux_recv, aux_s, aux_r, s)
-            learn(aux_recv, s)
+            learn(aux_recv, wait_from(aux_send, aux_recv, aux_s, aux_r, d))
 
         learn(aux_send, me)
         each_peer(other)
@@ -449,12 +489,11 @@
 
     def home_sum(stage, half, total):
         src, dst, ssem, rsem = refs(stage, half)
-        total[...] = scatter_cols(src[me], home_hi[me], hot_home[me], home)
+        add_parts(total, scatter_cols(src[me], home_hi16[me], hot_home[me], home), rows, True)
 
         def other(d):
-            s = source(d)
-            wait_from(src, dst, ssem, rsem, s)
-            total[...] += scatter_cols(dst[s], home_hi[s], hot_home[s], home)
+            s = wait_from(src, dst, ssem, rsem, d)
+            add_parts(total, scatter_cols(dst[s], home_hi16[s], hot_home[s], home), rows)
 
         each_peer(other)
 
@@ -477,7 +516,7 @@
         src, dst, ssem, rsem = refs(stage + 1, half)
 
         def reply(d):
-            peer = lax.rem(me + d, peers)
+            peer = partner(d)
             src[peer] = gather_cols(h_table2[...], home_hi[peer], hot_home[peer], home, rows)
             to_peer(src, dst, ssem, rsem, d).start()
 
@@ -485,7 +524,7 @@
         dst[me] = gather_cols(h_table2[...], home_hi[me], hot_home[me], home, rows)
 
     def fetched(stage, half):
-        each_peer(lambda d: wait_from(*refs(stage, half), source(d)))
+        each_peer(lambda d: wait_from(*refs(stage, half), d))
         table_from(recv.at[stage, half], rows, n_table, n_table2)
 
     def operate_half(half):
@@ -498,8 +537,8 @@
 
         gather_elems(n_table2, pos_hi, hot_el, rows, visit)
         apply_operator(x_all, ws, wm, coef_q, rhs, terms)
-        scatter_elems(terms, pos_hi, hot_el, acc)
-        lay_out(send.at[2, half], acc, rows, 0)
+        scatter_elems(terms, pos_hi16, hot_el, acc)
+        lay_out(send.at[2, half], acc, rows)
         each_peer(lambda d: to_peer(*refs(2, half), d).start())
 
     def backs(half):
@@ -528,7 +567,7 @@
         gather_elems(n_table2, pos_hi, hot_el, rows, visit)
         ea[...] = dot3_nt(x3a[...], wa[0], wa[1])
         eb[...] = dot3_nt(x3b[...], wb[0], wb[1])
-        edge_scatter(ea, eb, emap_hi, hot_ed, rhs, e_acc.at[half])
+        edge_scatter(ea, eb, emap_hi16, hot_ed, rhs, e_acc.at[half])
         h = edges // CHUNK
         for side in range(2):
             for i in range(width // CHUNK):
@@ -540,11 +579,12 @@
             copy.start()
 
     restrict_half(0)
-    learn_home()
+    send_aux()
     restrict_half(1)
-    home_half(0, 0, False)
     keep_parts(ws, block_weights(stiff[...], 4))
     keep_parts(wm, block_weights(mass[...], 4))
+    learn_home()
+    home_half(0, 0, False)
     home_half(0, 1, False)
     operate_half(0)
     operate_half(1)
@@ -609,11 +649,17 @@
     half = rhs // 2
     rows = 3 * half
     scratch = [
+        ((rhs, edges), F32),
+        ((1, touched), jnp.int32),
+        ((1, touched), jnp.int32),
+        (pi.shape, F32),
+        (stiff.shape, F32),
+        (mass.shape, F32),
         ((2, rhs, width), F32),
         ((2, 2, half, width), F32),
         ((2, 2, half, width), F32),
-        ((peers, AUX, capacity), F32),
-        ((peers, AUX, capacity), F32),
+        ((peers, AUX // 2, capacity), F32),
+        ((peers, AUX // 2, capacity), F32),
         ((4, 2, peers, rows, capacity), F32),
         ((4, 2, peers, rows, capacity), F32),
         ((CHUNK, entries), BF16),
@@ -622,6 +668,9 @@
         ((1, ed * elems), jnp.int32),
         ((1, entries), jnp.int32),
         ((peers, 1, capacity), jnp.int32),
+        ((16, ed * elems), jnp.int16),
+        ((16, entries), jnp.int16),
+        ((peers, 16, capacity), jnp.int16),
         ((groups, CHUNK), F32),
         ((AUX, entries), F32),
         ((AUX, entries), F32),
@@ -650,12 +699,12 @@
         ((home * AUX, CHUNK), F32),
         ((2, e_groups * half, CHUNK), F32),
     ]
-    sems = [(2,), (2,), (peers,), (peers,), (4, 2, peers), (4, 2, peers), (2, 2), (2, 2)]
-    vmem = pl.BlockSpec(memory_space=pltpu.VMEM)
+    sems = [(2,), (2,), (peers,), (peers,), (4, 2, peers), (4, 2, peers), (2, 2), (2, 2), (6,)]
+    vmem, where = pl.BlockSpec(memory_space=pltpu.VMEM), pl.BlockSpec(memory_space=pl.ANY)
     return pl.pallas_call(
         functools.partial(kernel, grps, peers, home, e_groups),
         out_shape=jax.ShapeDtypeStruct((rhs, edges), F32),
-        in_specs=[vmem] * 9,
+        in_specs=[where, vmem, vmem, where, where, vmem, where, where, where],
         out_specs=vmem,
         scratch_shapes=[pltpu.VMEM(*s) for s in scratch]
         + [pltpu.SemaphoreType.DMA(s) for s in sems],

time: 127 us -> 120 us (0.945)
  Pallas kernels: 120 us -> 114 us
    pallas_call x1, Pallas kernels: 120 us -> 114 us  [per_device(): pl.pallas_call(functools.partial(kernel, grps, peers, home, e_groups), ou...]
    unnamed x13 -> x7, local copies, waits for them, and re-layouts: 3.02 us -> 2.35 us
where the time goes in v2:
time: 120 us; the launch traced here: 119 us
  Pallas kernels  114 us (95%)
  local copies, waits for them, and re-layouts  4.04 us (3%)
  other arithmetic  1.3 us (1%)
    pallas_call x1, Pallas kernels, per_device(): pl.pallas_call(functools.partial(kernel, grps, peers, home, e_groups), ou...  114 us

profile of v2, /device:TPU:0, one launch (start us, length us, event | category | flops | bytes accessed | tf_op | source)
XLA Modules:
  0.0 119.2 jit_solution(2561873540056194587)
XLA Ops:
  0.0 0.0 copy-start.1
  0.0 0.0 copy-start.2
  0.0 0.0 copy-start
  0.0 0.1 pad.2.clone
  0.1 0.6 copy-done.1
  0.7 0.0 copy-done.2
  0.7 0.7 maximum_maximum_fusion.coef
  1.3 0.8 copy.12
  2.2 0.7 reshape.11.local
  2.9 0.0 copy-done
  2.9 0.1 reshape.10
  3.0 0.6 pad_add_fusion.emap
  3.6 113.8 %shard_map.100 = f32[16,5376]{1,0:T(8,128)} custom-call(f32[16,5376]{1,0:T(8,128)} %res_in.1, s32[1,9216]{1,0:T(1,128)} %pad_add_fusion.emap, s32[1,4096]{1,0:T(1,128)} %reshape.11.local, s32[1,2048]{1,0:T(1,128)} %bitcast.17, s32[1,2048]{1,0:T(1,128)} %bitcast.18, f32[8,64]{1,0:T(8,128)} %maximum_maximum_fusion.coef, f32[144,192]{1,0:T(8,128)} %pi_in.1, ...), custom_call_target="tpu_custom_call" | custom-call | tf_op jit(solution)/shard_map/pallas_call | solution.py:704
  117.5 1.7 %copy.14 = f32[16,5376]{1,0:T(8,128)} copy(f32[16,5376]{1,0:T(8,128)} %shard_map.100) | data formatting | bytes 688128
  (3 shorter events, 0.0 us)
Async XLA Ops:
  0.0 0.7 copy-start.1
  0.0 0.7 copy-start.2
  0.0 2.9 %copy-start = (s32[144,64]{0,1:T(8,128)S(1)}, s32[144,64]{0,1:T(8,128)}, u32[]{:S(2)}) copy-start(s32[144,64]{0,1:T(8,128)} %param.16) | copy-start | bytes 110596

commit v3 on v2

--- a/solution.py
+++ b/solution.py
@@ -1,4 +1,5 @@
 import functools
+import math
 import jax
 import jax.numpy as jnp
 from jax import lax
@@ -12,6 +13,7 @@
 F32 = jnp.float32
 BF16 = jnp.bfloat16
 AUX = 8
+FULL = 4096.0
 CHEB_LOW = 0.3
 CHEB_HIGH = 2.0
 VMEM_BYTES = 60 * 1024 * 1024
@@ -162,15 +164,19 @@
     lax.fori_loop(0, coef_q.shape[1] // WIDE, body, 0)
 
 
-def prepare_places(peers, owner_ref, slot_ref, local_ref, pos_hi, pos_hi16, hot_el, slot_buf):
+def prepare_places(peers, capacity, spread, owner_ref, slot_ref, local_ref, pos_hi, pos_hi16, hot_el, slot_buf):
     touched = owner_ref.shape[1]
-    capacity = 2 * touched // peers
-    groups = 2 * touched // CHUNK
+    groups = slot_buf.shape[0]
+    per = -(-N_LOC // peers)
     tri = ones_where(iota((CHUNK, CHUNK), 0) < iota((CHUNK, CHUNK), 1))
     carry = jnp.zeros((peers, 1), F32)
-    place = []
+    place, kept = [], []
     for i in range(touched // CHUNK):
         own = owner_ref[:, i * CHUNK : (i + 1) * CHUNK]
+        slot = slot_ref[:, i * CHUNK : (i + 1) * CHUNK]
+        if spread:
+            own, slot = slot % peers, own * per + slot // peers
+        kept.append(slot + 1)
         hot = jnp.where(iota((peers, CHUNK), 0) == own, 1.0, 0.0)
         before = dot(hot.astype(BF16), tri) + carry
         rank = jnp.sum(hot * before, axis=0, keepdims=True)
@@ -184,13 +190,17 @@
         high, low = pos // CHUNK, pos % CHUNK
         table_hi = jnp.where(rows8 == i, high.astype(F32), table_hi)
         table_lo = jnp.where(rows8 == i, low.astype(F32), table_lo)
-        slot = slot_ref[:, i * CHUNK : (i + 1) * CHUNK] + 1
+        slot = kept[i]
         here = iota((groups, CHUNK), 0) == high
         s_hi = jnp.where(here, (slot // CHUNK).astype(F32), 0.0)
         s_lo = jnp.where(here, (slot % CHUNK).astype(F32), 0.0)
         both = jnp.concatenate([s_hi, s_lo], axis=0).astype(BF16)
         slots = slots + dot_nt(both, onehot(low))
-    slot_buf[...] = slots[:groups] * float(CHUNK) + slots[groups:]
+    numbers = slots[:groups] * float(CHUNK) + slots[groups:]
+    if spread:
+        most = jnp.max(carry, axis=0, keepdims=True)
+        numbers = numbers + jnp.where(most > float(capacity), FULL, 0.0)
+    slot_buf[...] = numbers
     table = jnp.concatenate([table_hi, table_lo], axis=0).astype(BF16)
 
     def body(i, _):
@@ -256,7 +266,7 @@
 def lay_out(send, acc, rows):
     _, kept, capacity = send.shape
     for h in range(acc.shape[0] // rows):
-        step = min(capacity, CHUNK)
+        step = math.gcd(capacity, CHUNK)
         for s in range(CHUNK // step):
             lane = h * CHUNK + s * step
             peer, off = lane // capacity, lane % capacity
@@ -268,7 +278,7 @@
 def table_from(got, rows, table, table2):
     peers, _, capacity = got.shape
     for h in range(peers * capacity // CHUNK):
-        step = min(capacity, CHUNK)
+        step = math.gcd(capacity, CHUNK)
         parts = []
         for s in range(CHUNK // step):
             lane = h * CHUNK + s * step
@@ -334,16 +344,16 @@
 
 
 def kernel(
-    grps, peers, home, e_groups,
+    grps, peers, home, e_groups, capacity, spread,
     res_in, emap, local, owner_in, slot_in, coef, pi_in, stiff_in, mass_in,
-    out,
+    out, flag_out,
     res, owner, slot, pi, stiff, mass,
     rim_in, rim_out, rim_back, aux_send, aux_recv, send, recv,
     hot_el, hot_ed, hot_home, emap_hi, pos_hi, home_hi,
     emap_hi16, pos_hi16, home_hi16, slot_buf, coef_q, diag_q,
     wa, wb, ws, wm, e_table, e_table2, xa, xb, x3a, x3b, ea, eb, terms,
-    n_table, n_table2, x_all, acc, acc_d, h_table, h_table2, rhs_nodes, h_acc, floored, e_acc,
-    rim_s, rim_r, aux_s, aux_r, x_s, x_r, back_s, back_r, in_s,
+    n_table, n_table2, x_all, acc, acc_d, h_table, h_table2, rhs_nodes, h_acc, floored, e_acc, flag, flag_in,
+    rim_s, rim_r, aux_s, aux_r, x_s, x_r, back_s, back_r, in_s, flag_s, flag_r,
 ):
     grp, me = lax.axis_index("grp"), lax.axis_index("dev")
     rhs = res.shape[0] // 2
@@ -409,9 +419,14 @@
         )
 
     each_peer(greet)
-    for device in (before_id, after_id):
+    others = [(lax.rem(grp + d, grps), me) for d in range(1, grps)]
+    for device in [before_id, after_id] + others:
         pl.semaphore_signal(barrier, 1, device_id=device, device_id_type=pl.DeviceIdType.MESH)
-    pl.semaphore_wait(barrier, peers + 1)
+    pl.semaphore_wait(barrier, peers + grps)
+    flags = [
+        remote(flag, flag_in.at[i], flag_s.at[i], flag_r.at[i], device)
+        for i, device in enumerate(others)
+    ]
 
     rims = [
         remote(res_in.at[:, edges - width :], rim_in.at[0], rim_s.at[0], rim_r.at[0], after_id),
@@ -422,7 +437,9 @@
 
     loads[0].wait()
     loads[1].wait()
-    prepare_places(peers, owner, slot, local, pos_hi, pos_hi16, hot_el, slot_buf)
+    prepare_places(
+        peers, capacity, spread, owner, slot, local, pos_hi, pos_hi16, hot_el, slot_buf
+    )
     loads[2].wait()
     nodes = stiff.shape[0]
     keep_parts(wa, pi_weights(pi[:128], 2, nodes))
@@ -469,9 +486,12 @@
 
     def learn_home():
         floored[...] = jnp.zeros_like(floored)
+        flag[...] = jnp.zeros_like(flag)
 
         def learn(got, s):
-            high, low = home_index(got[s, 3:4, :])
+            row = got[s, 3:4, :]
+            flag[...] = jnp.maximum(flag[...], jnp.max(row, axis=1, keepdims=True))
+            high, low = home_index(row)
             hot = onehot(low)
             home_hi[s] = high
             hot_home[s] = hot
@@ -486,6 +506,8 @@
         learn(aux_send, me)
         each_peer(other)
         floored[...] = jnp.maximum(floored[...], 1.0)
+        for copy in flags:
+            copy.start()
 
     def home_sum(stage, half, total):
         src, dst, ssem, rsem = refs(stage, half)
@@ -607,7 +629,12 @@
                 value = value + rim_back[half, 1, :, at : at + CHUNK]
             out[mine, h * CHUNK : (h + 1) * CHUNK] = value
 
-    for copy in rims + backs(0) + backs(1):
+    worst = flag[...]
+    for i, copy in enumerate(flags):
+        copy.wait_recv()
+        worst = jnp.maximum(worst, flag_in[i])
+    flag_out[...] = worst
+    for copy in rims + backs(0) + backs(1) + flags:
         copy.wait_send()
 
     def sent(d):
@@ -627,10 +654,8 @@
     nodes = local_map.shape[0]
     touched = node_owner.shape[0]
     peers, grps = lax.axis_size("dev"), lax.axis_size("grp")
-    capacity = 2 * touched // peers
     rim = edges // 8
     width = -(-rim // CHUNK) * CHUNK
-    entries = nodes * elems
     place = edge_map.T - rim
     place = jnp.where(
         place < 0,
@@ -640,7 +665,25 @@
     emap = jnp.concatenate([place[:, :128].reshape(1, -1), place[:, 128:].reshape(1, -1)], axis=1)
     local = local_map.T.reshape(1, -1)
     coef = jnp.concatenate([curl[None], permittivity, jnp.zeros((1, elems), F32)], axis=0)
-    groups = 2 * touched // CHUNK
+    args = (residual, emap, local, node_owner[None], node_slot[None], coef, pi, stiff, mass)
+    most = 2 * touched // peers
+    usual = -(-(3 * touched // (2 * peers)) // 128) * 128
+    if usual >= most:
+        return run(grps, peers, ed, elems, nodes, touched, most, False, args)[0]
+    result, flag = run(grps, peers, ed, elems, nodes, touched, usual, True, args)
+
+    def with_room(result, *args):
+        return run(grps, peers, ed, elems, nodes, touched, most, False, args)[0]
+
+    return lax.cond(flag[0, 0] >= FULL, with_room, lambda result, *args: result, result, *args)
+
+
+def run(grps, peers, ed, elems, nodes, touched, capacity, spread, args):
+    residual, pi, stiff, mass = args[0], args[6], args[7], args[8]
+    rhs, edges = residual.shape
+    width = -(-(edges // 8) // CHUNK) * CHUNK
+    entries = nodes * elems
+    groups = peers * capacity // CHUNK
     home = -(-N_LOC // CHUNK)
     home_even = home + home % 2
     e_groups = (edges + 2 * width) // CHUNK
@@ -698,20 +741,24 @@
         ((home * rows, CHUNK), F32),
         ((home * AUX, CHUNK), F32),
         ((2, e_groups * half, CHUNK), F32),
+        ((8, 128), F32),
+        ((grps - 1, 8, 128), F32),
     ]
-    sems = [(2,), (2,), (peers,), (peers,), (4, 2, peers), (4, 2, peers), (2, 2), (2, 2), (6,)]
+    sems = [(2,), (2,), (peers,), (peers,), (4, 2, peers), (4, 2, peers), (2, 2), (2, 2), (6,), (grps - 1,), (grps - 1,)]
     vmem, where = pl.BlockSpec(memory_space=pltpu.VMEM), pl.BlockSpec(memory_space=pl.ANY)
     return pl.pallas_call(
-        functools.partial(kernel, grps, peers, home, e_groups),
-        out_shape=jax.ShapeDtypeStruct((rhs, edges), F32),
+        functools.partial(kernel, grps, peers, home, e_groups, capacity, spread),
+        out_shape=[
+            jax.ShapeDtypeStruct((rhs, edges), F32), jax.ShapeDtypeStruct((8, 128), F32)
+        ],
         in_specs=[where, vmem, vmem, where, where, vmem, where, where, where],
-        out_specs=vmem,
+        out_specs=[vmem, vmem],
         scratch_shapes=[pltpu.VMEM(*s) for s in scratch]
         + [pltpu.SemaphoreType.DMA(s) for s in sems],
         compiler_params=pltpu.CompilerParams(
-            collective_id=0, has_side_effects=True, vmem_limit_bytes=VMEM_BYTES
+            collective_id=0 if spread else 1, has_side_effects=True, vmem_limit_bytes=VMEM_BYTES
         ),
-    )(residual, emap, local, node_owner[None], node_slot[None], coef, pi, stiff, mass)
+    )(*args)
 
 
 def solution(mesh):

time: 120 us -> 106 us (0.88)
  Pallas kernels: 114 us -> 99.1 us
    pallas_call x1, Pallas kernels: 114 us -> 99.1 us  [run(): pl.pallas_call(functools.partial(kernel, grps, peers, home, e_groups, cap...]
where the time goes in v3:
time: 106 us
  Pallas kernels  99.1 us (93%)
  local copies, waits for them, and re-layouts  3.78 us (4%)
  other arithmetic  1.66 us (2%)
    pallas_call x1, Pallas kernels, run(): pl.pallas_call(functools.partial(kernel, grps, peers, home, e_groups, cap...  99.1 us

profile of v3, /device:TPU:0, one launch (start us, length us, event | category | flops | bytes accessed | tf_op | source)
XLA Modules:
  0.0 105.5 jit_solution(6540588777974196943)
XLA Ops:
  0.0 0.0 copy-start
  0.0 0.1 pad.2.clone
  0.1 0.8 maximum_maximum_fusion.coef
  0.9 0.8 copy.14
  1.7 0.1 reshape.15.local
  1.8 0.9 fusion
  2.7 0.0 copy-start.1
  2.7 0.1 reshape.14
  2.8 0.0 copy-start.4
  2.8 0.0 copy-start.5
  2.8 0.0 copy-done
  2.8 0.8 copy-done.1
  3.6 0.0 copy-done.4
  3.6 0.0 copy-done.5
  3.6 0.0 copy-start.2
  3.6 0.0 copy-start.3
  3.6 99.1 %shard_map.102 = (f32[16,5376]{1,0:T(8,128)S(1)}, f32[8,128]{1,0:T(8,128)}) custom-call(f32[16,5376]{1,0:T(8,128)S(1)} %copy-done, s32[1,9216]{1,0:T(1,128)S(1)} %pad_add_fusion.emap, s32[1,4096]{1,0:T(1,128)S(1)} %reshape.15.local, s32[1,2048]{1,0:T(1,128)S(1)} %bitcast.17, s32[1,2048]{1,0:T(1,128)S(1)} %bitcast.19, f32[8,64]{1,0:T(8,128)S(1)} %maximum_maximum_fusion.coef, ...), custom_call_target="tpu_custom_call" | custom-call | tf_op jit(solution)/shard_map/pallas_call | solution.py:749
  102.7 1.2 %slice.11 = f32[1,1]{1,0:T(1,128)} slice(f32[8,128]{1,0:T(8,128)} %get-tuple-element.39), slice={[0:1], [0:1]} | slice | bytes 8 | tf_op jit(solution)/shard_map/slice | solution.py:678
  104.6 0.0 copy-done.2
  104.6 0.0 copy-done.3
  104.6 0.2 conditional.1
  104.8 0.7 copy.18
  (3 shorter events, 0.0 us)
Async XLA Ops:
  0.0 2.8 %copy-start = (f32[16,5376]{1,0:T(8,128)S(1)}, f32[16,5376]{1,0:T(8,128)}, u32[]{:S(2)}) copy-start(f32[16,5376]{1,0:T(8,128)} %res_in.1) | copy-start | bytes 1032196
  2.7 0.9 copy-start.1
  2.8 0.8 copy-start.4
  2.8 0.8 copy-start.5
  3.6 101.0 %copy-start.2 = (f32[64,64]{1,0:T(8,128)S(1)}, f32[64,64]{1,0:T(8,128)}, u32[]{:S(2)}) copy-start(f32[64,64]{1,0:T(8,128)} %stiff_in.1) | copy-start | bytes 49156
  3.6 101.0 %copy-start.3 = (f32[64,64]{1,0:T(8,128)S(1)}, f32[64,64]{1,0:T(8,128)}, u32[]{:S(2)}) copy-start(f32[64,64]{1,0:T(8,128)} %mass_in.1) | copy-start | bytes 49156
